TPU v7x, 32 devices: a whole 2x2x4 slice. The times are simulated.
32 devices in a mesh: node: 16 (over z, x, core), grp: 2 (over y).
Axes of the slice: x: 2, y: 2, z: 4, core: 2. Of those that a mesh axis runs over, the one named last changes fastest.
Arguments:
- samples: bfloat16 [16384, 2048], P(('node', 'grp')), may hold values from -6 to 6
- diag_block: bfloat16 [16384, 1024], P(('node', 'grp')), may hold values from -0.1875 to 0.1875
- test_matrix: bfloat16 [16384, 2048], P('node'), may hold values from -6 to 6
- coeffs: bfloat16 [16384, 256], P(('node', 'grp')), may hold values from -0.1875 to 0.1875
- cross: bfloat16 [4096, 256], P('node'), may hold values from -0.375 to 0.375
- skeleton: int32 [16, 256], P('node'), may hold values from 0 to 1023, as said below
- counts: int32 [16], P('node'), may hold values from 64 to 256, as said below
- parent_slot: int32 [16], P('node'), may hold values from 0 to 1, as said below
Outputs:
- generators: bfloat16 [4096, 2048], P(('node', 'grp'))
- parent_samples: float32 [8192, 2048], P(('node', 'grp'))
Inputs may be any that keep to these rules, and one draw needn't show every extreme that they name: Each row holds 256 distinct rows of the node; the first counts of them are its skeleton, the rest are ignored. `counts`: some node has exactly 256. `parent_slot`: two siblings hold different values.
All inputs are finite; a program needn't handle non-finite values.
Results may differ from a plain program's by a relative error of at most 0.006.
Values may be sent and summed in bfloat16 or wider, within the bound.
No kernel may reach another device: no remote copies, remote signals or barrier semaphores. Data moves between devices by JAX's collectives and lax.ppermute only.
A program may use at most 64 MiB of HBM per device.

v0:
```python
import functools

import jax
import jax.numpy as jnp
from jax import lax
from jax.experimental import pallas as pl
from jax.experimental.pallas import tpu as pltpu
from jax.sharding import PartitionSpec as P

SIB_BIT = 2
CHUNKS = 4
BLOCK = 256
READY = 2
DEAD = 2.0**20
F32, BF16, I32 = jnp.float32, jnp.bfloat16, jnp.int32

VMEM = pl.BlockSpec(memory_space=pltpu.VMEM)
SMEM = pl.BlockSpec(memory_space=pltpu.SMEM)
HBM = pl.BlockSpec(memory_space=pltpu.HBM)
ANY = pl.BlockSpec(memory_space=pl.ANY)
like = jax.ShapeDtypeStruct


def swap(block, axis, distance):
    count = lax.axis_size(axis)
    route = []
    for low in range(count):
        high = low | 1 << distance
        if high != low and high < count:
            route += [(low, high), (high, low)]
    return lax.ppermute(block, axis, route)


def call(body, outs, in_specs, out_specs, operands, scratch=(), flops=0, moved=0, alias=None, limit=24):
    return pl.pallas_call(
        body,
        name=getattr(body, "func", body).__name__,
        out_shape=outs,
        in_specs=in_specs,
        out_specs=out_specs,
        scratch_shapes=list(scratch),
        input_output_aliases=alias or {},
        compiler_params=pltpu.CompilerParams(vmem_limit_bytes=limit * 2**20),
        cost_estimate=pl.CostEstimate(flops=flops, bytes_accessed=moved, transcendentals=0),
    )(*operands)


def mm(a, b):
    return jnp.dot(a, b, preferred_element_type=F32)


def hot_rows(skel, rows):
    slots = skel.shape[1]
    down = jnp.broadcast_to(skel, (128, slots)).T
    lane = lax.broadcasted_iota(I32, (slots, 128), 1)
    parts = [jnp.where(down == lane + at, 1.0, 0.0).astype(BF16) for at in range(0, rows, 128)]
    return jnp.concatenate(parts, axis=1)


def turned(coeffs):
    return coeffs.astype(F32).T.astype(BF16)


def is_owner(meta_ref):
    return jnp.max(meta_ref[0:1, :]) > 0


def alive_rows(meta_ref, shape, first=0):
    return lax.broadcasted_iota(I32, shape, 0) + first < jnp.max(meta_ref[1:2, :])


def own_half(group, half):
    return pl.ds(pl.multiple_of(group * half, half), half)


def first_body(slot_ref, skel_ref, coeffs_ref, cross_ref, diag_ref, samples_ref, tests_ref,
               message_ref, hot_ref, diag_rows_ref, meta_ref, cross_out_ref,
               skel_buf, coeffs_buf, diag_buf, samples_buf, tests_buf, sems):
    group = lax.axis_index("grp")
    half = coeffs_ref.shape[0]
    width = samples_buf.shape[1]
    pairs = [(skel_ref, skel_buf), (diag_ref, diag_buf), (samples_ref.at[:, pl.ds(0, width)], samples_buf),
             (tests_ref.at[:, pl.ds(0, width)], tests_buf), (coeffs_ref, coeffs_buf), (cross_ref, cross_out_ref)]
    copies = [pltpu.make_async_copy(src, dst, sems.at[i]) for i, (src, dst) in enumerate(pairs)]
    for copy in copies:
        copy.start()
    owner = slot_ref[0] == group
    meta_ref[...] = jnp.zeros(meta_ref.shape, I32) + jnp.where(owner, 1, 0)
    copies[0].wait()
    hot = hot_rows(skel_buf[...], 2 * half)
    hot_ref[...] = hot
    copies[1].wait()
    mine = hot_ref[:, own_half(group, half)]
    diag_rows = (-mm(mine, diag_buf[...])).astype(BF16)
    diag_rows_ref[...] = diag_rows
    for copy in copies[2:]:
        copy.wait()

    @pl.when(owner)
    def _():
        message_ref[...] = turned(coeffs_buf[...])

    @pl.when(jnp.logical_not(owner))
    def _():
        for at in range(0, width, BLOCK):
            cut = slice(at, at + BLOCK)
            message_ref[:, cut] = (mm(mine, samples_buf[:, cut]) + mm(diag_rows, tests_buf[:, cut])).astype(BF16)


def skel_rows(group, out_ref, first, hot_ref, diag_rows_ref, samples_ref, tests_ref):
    half = samples_ref.shape[0]
    mine = hot_ref[:, own_half(group, half)]
    for at in range(0, out_ref.shape[1], BLOCK):
        cut = slice(first + at, first + at + BLOCK)
        out_ref[:, at:at + BLOCK] = (
            mm(mine, samples_ref[:, cut]) + mm(diag_rows_ref[...], tests_ref[:, cut])).astype(BF16)


def next_body(owner_ref, count_ref, coeffs_ref, hot_ref, diag_rows_ref, samples_ref, tests_ref,
              own_ref, second_ref, partial_ref, slots_ref, meta_ref, coeffs_buf, sem):
    group = lax.axis_index("grp")
    half = coeffs_ref.shape[0]
    width = own_ref.shape[1]
    copy = pltpu.make_async_copy(coeffs_ref, coeffs_buf, sem)
    copy.start()
    owner = is_owner(owner_ref)
    meta_ref[0:1, :] = owner_ref[0:1, :]
    meta_ref[1:2, :] = jnp.zeros((1, 128), I32) + count_ref[0]
    skel_rows(group, second_ref, width, hot_ref, diag_rows_ref, samples_ref, tests_ref)
    copy.wait()

    @pl.when(owner)
    def _():
        skel_rows(group, own_ref, 0, hot_ref, diag_rows_ref, samples_ref, tests_ref)

    @pl.when(jnp.logical_not(owner))
    def _():
        slots = turned(coeffs_buf[...])
        slots_ref[...] = slots
        for at in range(0, width, BLOCK):
            cut = slice(at, at + BLOCK)
            partial_ref[:, cut] = mm(slots, tests_ref[own_half(group, half), cut]) + mm(hot_ref[...], tests_ref[:, cut])


def rest_body(meta_ref, slots_ref, hot_ref, diag_rows_ref, samples_ref, tests_ref, *outs):
    group = lax.axis_index("grp")
    others_ref = outs[-1]
    share = others_ref.shape[0]
    for i, out_ref in enumerate(outs[:-1]):
        skel_rows(group, out_ref, (i + 2) * out_ref.shape[1], hot_ref, diag_rows_ref, samples_ref, tests_ref)

    @pl.when(is_owner(meta_ref))
    def _():
        others_ref[...] = jnp.zeros(others_ref.shape, BF16)

    @pl.when(jnp.logical_not(is_owner(meta_ref)))
    def _():
        others_ref[...] = slots_ref[own_half(1 - group, share), :]


def send_body(index, meta_ref, first_got_ref, own_ref, got_ref, partial_ref, slots_ref, hot_ref, tests_ref, *rest):
    out_ref = rest[-1]
    group = lax.axis_index("grp")
    cap, width = out_ref.shape
    half = tests_ref.shape[0] // 2
    owner = is_owner(meta_ref)
    alive = alive_rows(meta_ref, (cap, BLOCK))

    @pl.when(owner)
    def _():
        for at in range(0, width, BLOCK):
            cut = slice(at, at + BLOCK)
            out_ref[:, cut] = jnp.where(alive, own_ref[:, cut].astype(F32) + got_ref[:, cut].astype(F32), DEAD).astype(BF16)

    @pl.when(jnp.logical_not(owner))
    def _():
        for at in range(0, width, BLOCK):
            cut = slice(index * width + at, index * width + at + BLOCK)
            part = mm(first_got_ref[...], tests_ref[own_half(1 - group, half), cut])
            if index == 0:
                part += partial_ref[:, cut]
            elif index >= CHUNKS - READY:
                place = index * width + at - (CHUNKS - READY) * width
                part += partial_ref[:, place:place + BLOCK]
            else:
                part += mm(slots_ref[...], tests_ref[own_half(group, half), cut]) + mm(hot_ref[...], tests_ref[:, cut])
            out_ref[:, at:at + BLOCK] = jnp.where(alive, part, 0.0).astype(BF16)


def early_body(meta_ref, hot_ref, message_ref, slots_ref, tests_ref, share_ref, partial_ref):
    group = lax.axis_index("grp")
    share, cols = share_ref.shape
    half = tests_ref.shape[0] // 2
    first = cols - partial_ref.shape[1]
    owner = is_owner(meta_ref)
    rows = own_half(group, share)

    @pl.when(owner)
    def _():
        for at in range(0, cols, BLOCK):
            cut = slice(at, at + BLOCK)
            share_ref[:, cut] = (mm(message_ref[rows, :], tests_ref[own_half(group, half), cut])
                                 + mm(hot_ref[rows, :], tests_ref[:, cut]))

    @pl.when(jnp.logical_not(owner))
    def _():
        for at in range(first, cols, BLOCK):
            cut = slice(at, at + BLOCK)
            partial_ref[:, at - first:at - first + BLOCK] = (
                mm(slots_ref[...], tests_ref[own_half(group, half), cut]) + mm(hot_ref[...], tests_ref[:, cut]))


def generator_body(meta_ref, share_ref, others_ref, tests_ref, *rest):
    sent = rest[:CHUNKS]
    out_ref, token_ref, buf, sems = rest[CHUNKS + 1:]
    token_ref[...] = jnp.zeros(token_ref.shape, I32)
    group = lax.axis_index("grp")
    share, cols = out_ref.shape
    half = tests_ref.shape[0] // 2
    width = cols // CHUNKS
    owner = is_owner(meta_ref)
    rows = own_half(group, share)
    copies = [pltpu.make_async_copy(buf.at[:, pl.ds(i * width, width)], out_ref.at[:, pl.ds(i * width, width)], sems.at[i])
              for i in range(CHUNKS)]

    @pl.when(owner)
    def _():
        alive = alive_rows(meta_ref, (share, BLOCK), group * share)
        for i in range(CHUNKS):
            for at in range(i * width, (i + 1) * width, BLOCK):
                cut = slice(at, at + BLOCK)
                part = share_ref[:, cut] + mm(others_ref[...], tests_ref[own_half(1 - group, half), cut])
                buf[:, cut] = jnp.where(alive, part, 0.0).astype(BF16)
            copies[i].start()

    @pl.when(jnp.logical_not(owner))
    def _():
        for i in range(CHUNKS):
            buf[:, i * width:(i + 1) * width] = sent[i][rows, :]
            copies[i].start()

    for copy in copies:
        copy.wait()


def parent_body(index, token, meta_ref, cross_ref, cross_got_ref, sent_ref, got_ref, *rest):
    out_ref = rest[-3 - token]
    buf, sems = rest[-2:]
    if token:
        rest[-3][...] = jnp.zeros(rest[-3].shape, I32)
    width = sent_ref.shape[1]
    owner = is_owner(meta_ref)
    copies = [pltpu.make_async_copy(buf.at[:, pl.ds(at, BLOCK)], out_ref.at[:, pl.ds(index * width + at, BLOCK)],
                                    sems.at[at // BLOCK]) for at in range(0, width, BLOCK)]

    def work(skel_ref, rows_ref, gen_ref):
        for j, at in enumerate(range(0, width, BLOCK)):
            cut = pl.ds(at, BLOCK)
            skel = skel_ref[:, cut].astype(F32)
            buf[:, cut] = jnp.where(skel > DEAD / 2, 0.0, skel - mm(rows_ref[...], gen_ref[:, cut]))
            copies[j].start()

    @pl.when(owner)
    def _():
        work(sent_ref, cross_ref, got_ref)

    @pl.when(jnp.logical_not(owner))
    def _():
        work(got_ref, cross_got_ref, sent_ref)

    for copy in copies:
        copy.wait()


def local(samples, diag_block, test_matrix, coeffs, cross, skeleton, counts, parent_slot):
    half, cap = coeffs.shape
    rows, cols = test_matrix.shape
    share = cap // 2
    width = cols // CHUNKS
    dma = pltpu.SemaphoreType.DMA
    diag_far, coeffs_far, cross_far, skeleton_far, samples_far, tests_far = (
        pltpu.with_memory_space_constraint(x, pltpu.HBM)
        for x in (diag_block, coeffs, cross, skeleton, samples, test_matrix))
    piece = like((cap, width), BF16)

    message, hot, diag_rows, owner, cross_near = call(
        first_body,
        (piece, like((cap, rows), BF16), like((cap, rows), BF16), like((8, 128), I32), like((cap, cap), BF16)),
        [SMEM] + [HBM] * 6,
        (VMEM,) * 5,
        (parent_slot, skeleton_far, coeffs_far, cross_far, diag_far, samples_far, tests_far),
        [pltpu.VMEM((1, cap), I32), pltpu.VMEM((half, cap), BF16), pltpu.VMEM((half, rows), BF16),
         pltpu.VMEM((half, width), BF16), pltpu.VMEM((rows, width), BF16), dma((6,))],
        flops=2 * cap * rows * (half + width), moved=2 * (half * rows + (half + rows) * width),
    )
    got = [swap(message, "grp", 0)]
    cross_got = swap(cross_near, "node", SIB_BIT)
    own0, own1, partial, slots, meta = call(
        next_body,
        (piece, piece, like((cap, width), F32), like((cap, half), BF16), like((8, 128), I32)),
        [VMEM, SMEM, HBM] + [VMEM] * 4,
        (VMEM,) * 5,
        (owner, counts, coeffs_far, hot, diag_rows, samples, test_matrix),
        [pltpu.VMEM((half, cap), BF16), dma],
        flops=4 * cap * (rows + half) * width, moved=2 * (half + rows) * width,
    )
    got.append(swap(own1, "grp", 0))
    early, ready = call(
        early_body,
        (like((share, cols), F32), like((cap, READY * width), F32)),
        [VMEM] * 5,
        (VMEM, VMEM),
        (meta, hot, message, slots, test_matrix),
        flops=3 * share * rows * cols, moved=0,
    )
    *own, others = call(
        rest_body,
        (piece,) * (CHUNKS - 2) + (like((share, half), BF16),),
        [VMEM] * 6,
        (VMEM,) * (CHUNKS - 1),
        (meta, slots, hot, diag_rows, samples, test_matrix),
        flops=2 * cap * (rows + half) * width * (CHUNKS - 2), moved=2 * half * width,
    )
    own = [own0, own1] + own
    got += [swap(x, "grp", 0) for x in own[2:]]
    others_got = swap(others, "grp", 0)
    out = None
    sents = []
    tokens = []
    for i in range(CHUNKS):
        hold = (tokens[i - 2],) if i >= 2 else (cross_got,) if i == 1 else (ready,)
        sent = call(
            functools.partial(send_body, i),
            piece,
            [VMEM] * 8 + [ANY] * len(hold),
            VMEM,
            (meta, got[0], own[i], got[i], ready if i >= CHUNKS - READY else partial, slots, hot, test_matrix) + hold,
            flops=2 * cap * half * width * (1 if i == 0 else 4), moved=4 * cap * width,
        )
        sents.append(sent)
        arrived = swap(sent, "node", SIB_BIT)
        if i == CHUNKS - 1:
            generators, token = call(
                generator_body,
                (like((share, cols), BF16), like((8, 128), I32)),
                [VMEM] * (4 + CHUNKS) + [ANY],
                (HBM, VMEM),
                (meta, early, others_got, test_matrix, *sents, tokens[-1]),
                [pltpu.VMEM((share, cols), BF16), dma((CHUNKS,))],
                flops=4 * share * rows * cols, moved=2 * (rows + share) * cols,
            )
            tokens.append(token)
        token = i < CHUNKS - 1
        out, *more = call(
            functools.partial(parent_body, i, token),
            [like((cap, cols), F32)] + [like((8, 128), I32)] * token,
            [VMEM] * 5 + ([] if out is None else [HBM]) + [ANY] * (not token),
            [HBM] + [VMEM] * token,
            (meta, cross_near, cross_got, sent, arrived) + (() if out is None else (out,)) + tuple(tokens[-1:] * (not token)),
            [pltpu.VMEM((cap, width), F32), dma((width // BLOCK,))],
            flops=2 * cap * cap * width, moved=8 * cap * width,
            alias=None if out is None else {5: 0},
        )
        tokens += more
    return generators, out


def solution(mesh):
    return jax.shard_map(
        local,
        mesh=mesh,
        in_specs=(
            P(("node", "grp"), None),
            P(("node", "grp"), None),
            P("node", None),
            P(("node", "grp"), None),
            P("node", None),
            P("node", None),
            P("node"),
            P("node"),
        ),
        out_specs=(P(("node", "grp"), None), P(("node", "grp"), None)),
        check_vma=False,
    )
```

profile of v0, /device:TPU:0, one launch (start us, length us, event | category | flops | bytes accessed | tf_op | source)
XLA Modules:
  0.0 40.1 jit_solution(1173566327373413253)
XLA Ops:
  1.3 0.0 copy-start
  1.3 0.0 copy-start.1
  1.3 2.1 %first_body.1 = (bf16[256,512]{1,0:T(8,128)(2,1)S(1)}, bf16[256,1024]{1,0:T(8,128)(2,1)S(1)}, bf16[256,1024]{1,0:T(8,128)(2,1)S(1)}, s32[8,128]{1,0:T(8,128)S(1)}, bf16[256,256]{1,0:T(8,128)(2,1)S(1)}) custom-call(s32[1]{0:T(128)S(6)} %copy.17.slot_ref, s32[1,256]{1,0:T(1,128)} %skel_ref.1, bf16[512,256]{1,0:T(8,128)(2,1)} %coeffs_ref.3, ...), custom_call_target="tpu_custom_call" | custom-call | flops 536870912 | bytes 2621440 | tf_op jit(solution)/shard_map/first_body/pallas_call | solution.py:35
  3.4 3.5 %collective-permute-start.1 = (bf16[256,512]{1,0:T(8,128)(2,1)S(1)}, bf16[256,512]{1,0:T(8,128)(2,1)S(1)}, u32[]{:S(2)}, u32[]{:S(2)}) collective-permute-start(bf16[256,512]{1,0:T(8,128)(2,1)S(1)} %get-tuple-element.29.message_ref), channel_id=1, source_target_pairs={{0,1},{1,0},{2,3},{3,2},{4,5},{5,4},{6,7},{7,6},{8,9},{9,8},{10,11... | collective-permute-start | bytes 786440 | tf_op jit(solution)/shard_map/ppermute | solution.py:31
  7.6 0.0 copy-done
  7.6 0.0 copy-done.1
  7.6 1.5 %next_body.1 = (bf16[256,512]{1,0:T(8,128)(2,1)S(1)}, bf16[256,512]{1,0:T(8,128)(2,1)S(1)}, f32[256,512]{1,0:T(8,128)S(1)}, bf16[256,512]{1,0:T(8,128)(2,1)S(1)}, s32[8,128]{1,0:T(8,128)S(1)}) custom-call(s32[8,128]{1,0:T(8,128)S(1)} %get-tuple-element.25.owner_ref, s32[1]{0:T(128)S(6)} %copy.16.count_ref, bf16[512,256]{1,0:T(8,128)(2,1)} %coeffs_ref.3, ...), custom_call_target="tpu_custom_call" | custom-call | flops 805306368 | bytes 1572864 | tf_op jit(solution)/shard_map/next_body/pallas_call | solution.py:35
  9.1 0.5 %collective-permute-start.2 = (bf16[256,512]{1,0:T(8,128)(2,1)S(1)}, bf16[256,512]{1,0:T(8,128)(2,1)S(1)}, u32[]{:S(2)}, u32[]{:S(2)}) collective-permute-start(bf16[256,512]{1,0:T(8,128)(2,1)S(1)} %get-tuple-element.36.own_ref), channel_id=1, source_target_pairs={{0,1},{1,0},{2,3},{3,2},{4,5},{5,4},{6,7},{7,6},{8,9},{9,8},{10,11... | collective-permute-start | bytes 786440 | tf_op jit(solution)/shard_map/ppermute | solution.py:31
  9.7 1.6 %collective-permute-start.3 = (bf16[256,256]{1,0:T(8,128)(2,1)S(1)}, bf16[256,256]{1,0:T(8,128)(2,1)S(1)}, u32[]{:S(2)}, u32[]{:S(2)}) collective-permute-start(bf16[256,256]{1,0:T(8,128)(2,1)S(1)} %get-tuple-element.37.cross_ref), channel_id=1, source_target_pairs={{0,8},{8,0},{2,10},{10,2},{4,12},{12,4},{6,14},{14,6},{16,24},{24,... | collective-permute-start | bytes 393224 | tf_op jit(solution)/shard_map/ppermute | solution.py:31
  11.3 1.3 %early_body.1 = (f32[128,2048]{1,0:T(8,128)S(1)}, f32[256,1024]{1,0:T(8,128)S(1)}) custom-call(s32[8,128]{1,0:T(8,128)S(1)} %get-tuple-element.28.meta_ref, bf16[256,1024]{1,0:T(8,128)(2,1)S(1)} %get-tuple-element.26.hot_ref, bf16[256,512]{1,0:T(8,128)(2,1)S(1)} %get-tuple-element.29.message_ref, bf16[256,512]{1,0:T(8,128)(2,1)S(1)} %get-tuple-element.30.slots_ref, ...), custom_call_target="tpu_custom_call" | custom-call | flops 805306368 | tf_op jit(solution)/shard_map/early_body/pallas_call | solution.py:35
  12.6 1.5 %collective-permute-done.1.first_got_ref.got_ref = bf16[256,512]{1,0:T(8,128)(2,1)S(1)} collective-permute-done((bf16[256,512]{1,0:T(8,128)(2,1)S(1)}, bf16[256,512]{1,0:T(8,128)(2,1)S(1)}, u32[]{:S(2)}, u32[]{:S(2)}) %collective-permute-start.1) | collective-permute-done | bytes 262176 | tf_op jit(solution)/shard_map/ppermute | solution.py:31
  14.0 0.3 send_body.4.sent_ref.rest_0_
  14.3 2.4 %collective-permute-start.5 = (bf16[256,512]{1,0:T(8,128)(2,1)S(1)}, bf16[256,512]{1,0:T(8,128)(2,1)S(1)}, u32[]{:S(2)}, u32[]{:S(2)}) collective-permute-start(bf16[256,512]{1,0:T(8,128)(2,1)S(1)} %send_body.4.sent_ref.rest_0_), channel_id=1, source_target_pairs={{0,8},{8,0},{2,10},{10,2},{4,12},{12,4},{6,14},{14,6},{16,24},{24,... | collective-permute-start | bytes 786440 | tf_op jit(solution)/shard_map/ppermute | solution.py:31
  16.8 1.2 %rest_body.1 = (bf16[256,512]{1,0:T(8,128)(2,1)S(1)}, bf16[256,512]{1,0:T(8,128)(2,1)S(1)}, bf16[128,512]{1,0:T(8,128)(2,1)S(1)}) custom-call(s32[8,128]{1,0:T(8,128)S(1)} %get-tuple-element.28.meta_ref, bf16[256,512]{1,0:T(8,128)(2,1)S(1)} %get-tuple-element.30.slots_ref, bf16[256,1024]{1,0:T(8,128)(2,1)S(1)} %get-tuple-element.26.hot_ref, ...), custom_call_target="tpu_custom_call" | custom-call | flops 805306368 | bytes 524288 | tf_op jit(solution)/shard_map/rest_body/pallas_call | solution.py:35
  18.0 0.9 %collective-permute-start.4 = (bf16[256,512]{1,0:T(8,128)(2,1)S(1)}, bf16[256,512]{1,0:T(8,128)(2,1)S(1)}, u32[]{:S(2)}, u32[]{:S(2)}) collective-permute-start(bf16[256,512]{1,0:T(8,128)(2,1)S(1)} %get-tuple-element.38.own_ref), channel_id=1, source_target_pairs={{0,1},{1,0},{2,3},{3,2},{4,5},{5,4},{6,7},{7,6},{8,9},{9,8},{10,11... | collective-permute-start | bytes 786440 | tf_op jit(solution)/shard_map/ppermute | solution.py:31
  18.9 0.0 collective-permute-done.3.rest_0_.cross_got_ref
  18.9 0.5 %collective-permute-done.2.got_ref = bf16[256,512]{1,0:T(8,128)(2,1)S(1)} collective-permute-done((bf16[256,512]{1,0:T(8,128)(2,1)S(1)}, bf16[256,512]{1,0:T(8,128)(2,1)S(1)}, u32[]{:S(2)}, u32[]{:S(2)}) %collective-permute-start.2) | collective-permute-done | bytes 262176 | tf_op jit(solution)/shard_map/ppermute | solution.py:31
  19.4 0.3 send_body.5.sent_ref.rest_1_
  19.7 3.0 %collective-permute-start.7 = (bf16[256,512]{1,0:T(8,128)(2,1)S(1)}, bf16[256,512]{1,0:T(8,128)(2,1)S(1)}, u32[]{:S(2)}, u32[]{:S(2)}) collective-permute-start(bf16[256,512]{1,0:T(8,128)(2,1)S(1)} %send_body.5.sent_ref.rest_1_), channel_id=1, source_target_pairs={{0,8},{8,0},{2,10},{10,2},{4,12},{12,4},{6,14},{14,6},{16,24},{24,... | collective-permute-start | bytes 786440 | tf_op jit(solution)/shard_map/ppermute | solution.py:31
  22.8 0.5 %collective-permute-start.6 = (bf16[256,512]{1,0:T(8,128)(2,1)S(1)}, bf16[256,512]{1,0:T(8,128)(2,1)S(1)}, u32[]{:S(2)}, u32[]{:S(2)}) collective-permute-start(bf16[256,512]{1,0:T(8,128)(2,1)S(1)} %get-tuple-element.40.own_ref), channel_id=1, source_target_pairs={{0,1},{1,0},{2,3},{3,2},{4,5},{5,4},{6,7},{7,6},{8,9},{9,8},{10,11... | collective-permute-start | bytes 786440 | tf_op jit(solution)/shard_map/ppermute | solution.py:31
  23.2 0.0 collective-permute-done.5.got_ref
  23.2 1.3 %parent_body.4 = (f32[256,2048]{1,0:T(8,128)}, s32[8,128]{1,0:T(8,128)S(1)}) custom-call(s32[8,128]{1,0:T(8,128)S(1)} %get-tuple-element.28.meta_ref, bf16[256,256]{1,0:T(8,128)(2,1)S(1)} %get-tuple-element.37.cross_ref, bf16[256,256]{1,0:T(8,128)(2,1)S(1)} %collective-permute-done.3.rest_0_.cross_got_ref, bf16[256,512]{1,0:T(8,128)(2,1)S(1)} %send_body.4.sent_ref.rest_0_, ...), custom_call_target="tpu_custom_call" | custom-call | flops 67108864 | bytes 1048576 | tf_op jit(solution)/shard_map/parent_body/pallas_call | solution.py:35
  24.5 1.4 %collective-permute-done.4.got_ref = bf16[256,512]{1,0:T(8,128)(2,1)S(1)} collective-permute-done((bf16[256,512]{1,0:T(8,128)(2,1)S(1)}, bf16[256,512]{1,0:T(8,128)(2,1)S(1)}, u32[]{:S(2)}, u32[]{:S(2)}) %collective-permute-start.4) | collective-permute-done | bytes 262176 | tf_op jit(solution)/shard_map/ppermute | solution.py:31
  26.0 0.3 send_body.6.sent_ref.rest_2_
  26.3 1.7 %collective-permute-start.8 = (bf16[256,512]{1,0:T(8,128)(2,1)S(1)}, bf16[256,512]{1,0:T(8,128)(2,1)S(1)}, u32[]{:S(2)}, u32[]{:S(2)}) collective-permute-start(bf16[256,512]{1,0:T(8,128)(2,1)S(1)} %send_body.6.sent_ref.rest_2_), channel_id=1, source_target_pairs={{0,8},{8,0},{2,10},{10,2},{4,12},{12,4},{6,14},{14,6},{16,24},{24,... | collective-permute-start | bytes 786440 | tf_op jit(solution)/shard_map/ppermute | solution.py:31
  28.0 0.0 collective-permute-done.7.got_ref
  28.0 1.3 %parent_body.5 = (f32[256,2048]{1,0:T(8,128)}, s32[8,128]{1,0:T(8,128)S(1)}) custom-call(s32[8,128]{1,0:T(8,128)S(1)} %get-tuple-element.28.meta_ref, bf16[256,256]{1,0:T(8,128)(2,1)S(1)} %get-tuple-element.37.cross_ref, bf16[256,256]{1,0:T(8,128)(2,1)S(1)} %collective-permute-done.3.rest_0_.cross_got_ref, ...), custom_call_target="tpu_custom_call", output_to_operand_aliasing={{0}: (5, {})} | custom-call | flops 67108864 | bytes 1048576 | tf_op jit(solution)/shard_map/parent_body/pallas_call | solution.py:35
  29.3 0.8 %collective-permute-done.6.got_ref = bf16[256,512]{1,0:T(8,128)(2,1)S(1)} collective-permute-done((bf16[256,512]{1,0:T(8,128)(2,1)S(1)}, bf16[256,512]{1,0:T(8,128)(2,1)S(1)}, u32[]{:S(2)}, u32[]{:S(2)}) %collective-permute-start.6) | collective-permute-done | bytes 262176 | tf_op jit(solution)/shard_map/ppermute | solution.py:31
  30.1 0.3 send_body.7.rest_3_.sent_ref
  30.4 2.1 %collective-permute-start.9 = (bf16[256,512]{1,0:T(8,128)(2,1)S(1)}, bf16[256,512]{1,0:T(8,128)(2,1)S(1)}, u32[]{:S(2)}, u32[]{:S(2)}) collective-permute-start(bf16[256,512]{1,0:T(8,128)(2,1)S(1)} %send_body.7.rest_3_.sent_ref), channel_id=1, source_target_pairs={{0,8},{8,0},{2,10},{10,2},{4,12},{12,4},{6,14},{14,6},{16,24},{24,... | collective-permute-start | bytes 786440 | tf_op jit(solution)/shard_map/ppermute | solution.py:31
  32.5 0.9 %collective-permute-start = (bf16[128,512]{1,0:T(8,128)(2,1)S(1)}, bf16[128,512]{1,0:T(8,128)(2,1)S(1)}, u32[]{:S(2)}, u32[]{:S(2)}) collective-permute-start(bf16[128,512]{1,0:T(8,128)(2,1)S(1)} %get-tuple-element.32), channel_id=1, source_target_pairs={{0,1},{1,0},{2,3},{3,2},{4,5},{5,4},{6,7},{7,6},{8,9},{9,8},{10,11... | collective-permute-start | bytes 393224 | tf_op jit(solution)/shard_map/ppermute | solution.py:31
  33.3 0.0 collective-permute-done.8.got_ref
  33.3 1.3 %parent_body.6 = (f32[256,2048]{1,0:T(8,128)}, s32[8,128]{1,0:T(8,128)S(1)}) custom-call(s32[8,128]{1,0:T(8,128)S(1)} %get-tuple-element.28.meta_ref, bf16[256,256]{1,0:T(8,128)(2,1)S(1)} %get-tuple-element.37.cross_ref, bf16[256,256]{1,0:T(8,128)(2,1)S(1)} %collective-permute-done.3.rest_0_.cross_got_ref, ...), custom_call_target="tpu_custom_call", output_to_operand_aliasing={{0}: (5, {})} | custom-call | flops 67108864 | bytes 1048576 | tf_op jit(solution)/shard_map/parent_body/pallas_call | solution.py:35
  34.6 2.8 %collective-permute-done.others_ref = bf16[128,512]{1,0:T(8,128)(2,1)S(1)} collective-permute-done((bf16[128,512]{1,0:T(8,128)(2,1)S(1)}, bf16[128,512]{1,0:T(8,128)(2,1)S(1)}, u32[]{:S(2)}, u32[]{:S(2)}) %collective-permute-start) | collective-permute-done | bytes 131104 | tf_op jit(solution)/shard_map/ppermute | solution.py:31
  37.4 1.4 %generator_body.1 = (bf16[128,2048]{1,0:T(8,128)(2,1)}, s32[8,128]{1,0:T(8,128)S(1)}) custom-call(s32[8,128]{1,0:T(8,128)S(1)} %get-tuple-element.28.meta_ref, f32[128,2048]{1,0:T(8,128)S(1)} %get-tuple-element.31.share_ref, bf16[128,512]{1,0:T(8,128)(2,1)S(1)} %collective-permute-done.others_ref, bf16[1024,2048]{1,0:T(8,128)(2,1)S(1)} %copy-done, ...), custom_call_target="tpu_custom_call" | custom-call | flops 1073741824 | bytes 4718592 | tf_op jit(solution)/shard_map/generator_body/pallas_call | solution.py:35
  38.8 0.0 collective-permute-done.9.got_ref
  38.8 1.3 %parent_body.7 = f32[256,2048]{1,0:T(8,128)} custom-call(s32[8,128]{1,0:T(8,128)S(1)} %get-tuple-element.28.meta_ref, bf16[256,256]{1,0:T(8,128)(2,1)S(1)} %get-tuple-element.37.cross_ref, bf16[256,256]{1,0:T(8,128)(2,1)S(1)} %collective-permute-done.3.rest_0_.cross_got_ref, ...), custom_call_target="tpu_custom_call", output_to_operand_aliasing={{}: (5, {})} | custom-call | flops 67108864 | bytes 1048576 | tf_op jit(solution)/shard_map/parent_body/pallas_call | solution.py:35
Async XLA Ops:
  1.3 6.3 %copy-start = (bf16[1024,2048]{1,0:T(8,128)(2,1)S(1)}, bf16[1024,2048]{1,0:T(8,128)(2,1)}, u32[]{:S(2)}) copy-start(bf16[1024,2048]{1,0:T(8,128)(2,1)} %tests_ref.17) | copy-start | bytes 12582916
  1.3 6.3 %copy-start.1 = (bf16[512,2048]{1,0:T(8,128)(2,1)S(1)}, bf16[512,2048]{1,0:T(8,128)(2,1)}, u32[]{:S(2)}) copy-start(bf16[512,2048]{1,0:T(8,128)(2,1)} %samples_ref.5) | copy-start | bytes 6291460
  3.4 10.6 %collective-permute-start.1 = (bf16[256,512]{1,0:T(8,128)(2,1)S(1)}, bf16[256,512]{1,0:T(8,128)(2,1)S(1)}, u32[]{:S(2)}, u32[]{:S(2)}) collective-permute-start(bf16[256,512]{1,0:T(8,128)(2,1)S(1)} %get-tuple-element.29.message_ref), channel_id=1, source_target_pairs={{0,1},{1,0},{2,3},{3,2},{4,5},{5,4},{6,7},{7,6},{8,9},{9,8},{10,11... | collective-permute-start | bytes 786440 | tf_op jit(solution)/shard_map/ppermute | solution.py:31
  9.1 10.3 %collective-permute-start.2 = (bf16[256,512]{1,0:T(8,128)(2,1)S(1)}, bf16[256,512]{1,0:T(8,128)(2,1)S(1)}, u32[]{:S(2)}, u32[]{:S(2)}) collective-permute-start(bf16[256,512]{1,0:T(8,128)(2,1)S(1)} %get-tuple-element.36.own_ref), channel_id=1, source_target_pairs={{0,1},{1,0},{2,3},{3,2},{4,5},{5,4},{6,7},{7,6},{8,9},{9,8},{10,11... | collective-permute-start | bytes 786440 | tf_op jit(solution)/shard_map/ppermute | solution.py:31
  9.7 9.2 %collective-permute-start.3 = (bf16[256,256]{1,0:T(8,128)(2,1)S(1)}, bf16[256,256]{1,0:T(8,128)(2,1)S(1)}, u32[]{:S(2)}, u32[]{:S(2)}) collective-permute-start(bf16[256,256]{1,0:T(8,128)(2,1)S(1)} %get-tuple-element.37.cross_ref), channel_id=1, source_target_pairs={{0,8},{8,0},{2,10},{10,2},{4,12},{12,4},{6,14},{14,6},{16,24},{24,... | collective-permute-start | bytes 393224 | tf_op jit(solution)/shard_map/ppermute | solution.py:31
  14.3 8.9 %collective-permute-start.5 = (bf16[256,512]{1,0:T(8,128)(2,1)S(1)}, bf16[256,512]{1,0:T(8,128)(2,1)S(1)}, u32[]{:S(2)}, u32[]{:S(2)}) collective-permute-start(bf16[256,512]{1,0:T(8,128)(2,1)S(1)} %send_body.4.sent_ref.rest_0_), channel_id=1, source_target_pairs={{0,8},{8,0},{2,10},{10,2},{4,12},{12,4},{6,14},{14,6},{16,24},{24,... | collective-permute-start | bytes 786440 | tf_op jit(solution)/shard_map/ppermute | solution.py:31
  18.0 8.0 %collective-permute-start.4 = (bf16[256,512]{1,0:T(8,128)(2,1)S(1)}, bf16[256,512]{1,0:T(8,128)(2,1)S(1)}, u32[]{:S(2)}, u32[]{:S(2)}) collective-permute-start(bf16[256,512]{1,0:T(8,128)(2,1)S(1)} %get-tuple-element.38.own_ref), channel_id=1, source_target_pairs={{0,1},{1,0},{2,3},{3,2},{4,5},{5,4},{6,7},{7,6},{8,9},{9,8},{10,11... | collective-permute-start | bytes 786440 | tf_op jit(solution)/shard_map/ppermute | solution.py:31
  19.7 8.2 %collective-permute-start.7 = (bf16[256,512]{1,0:T(8,128)(2,1)S(1)}, bf16[256,512]{1,0:T(8,128)(2,1)S(1)}, u32[]{:S(2)}, u32[]{:S(2)}) collective-permute-start(bf16[256,512]{1,0:T(8,128)(2,1)S(1)} %send_body.5.sent_ref.rest_1_), channel_id=1, source_target_pairs={{0,8},{8,0},{2,10},{10,2},{4,12},{12,4},{6,14},{14,6},{16,24},{24,... | collective-permute-start | bytes 786440 | tf_op jit(solution)/shard_map/ppermute | solution.py:31
  22.8 7.3 %collective-permute-start.6 = (bf16[256,512]{1,0:T(8,128)(2,1)S(1)}, bf16[256,512]{1,0:T(8,128)(2,1)S(1)}, u32[]{:S(2)}, u32[]{:S(2)}) collective-permute-start(bf16[256,512]{1,0:T(8,128)(2,1)S(1)} %get-tuple-element.40.own_ref), channel_id=1, source_target_pairs={{0,1},{1,0},{2,3},{3,2},{4,5},{5,4},{6,7},{7,6},{8,9},{9,8},{10,11... | collective-permute-start | bytes 786440 | tf_op jit(solution)/shard_map/ppermute | solution.py:31
  26.3 7.1 %collective-permute-start.8 = (bf16[256,512]{1,0:T(8,128)(2,1)S(1)}, bf16[256,512]{1,0:T(8,128)(2,1)S(1)}, u32[]{:S(2)}, u32[]{:S(2)}) collective-permute-start(bf16[256,512]{1,0:T(8,128)(2,1)S(1)} %send_body.6.sent_ref.rest_2_), channel_id=1, source_target_pairs={{0,8},{8,0},{2,10},{10,2},{4,12},{12,4},{6,14},{14,6},{16,24},{24,... | collective-permute-start | bytes 786440 | tf_op jit(solution)/shard_map/ppermute | solution.py:31
  30.4 8.4 %collective-permute-start.9 = (bf16[256,512]{1,0:T(8,128)(2,1)S(1)}, bf16[256,512]{1,0:T(8,128)(2,1)S(1)}, u32[]{:S(2)}, u32[]{:S(2)}) collective-permute-start(bf16[256,512]{1,0:T(8,128)(2,1)S(1)} %send_body.7.rest_3_.sent_ref), channel_id=1, source_target_pairs={{0,8},{8,0},{2,10},{10,2},{4,12},{12,4},{6,14},{14,6},{16,24},{24,... | collective-permute-start | bytes 786440 | tf_op jit(solution)/shard_map/ppermute | solution.py:31
  32.5 5.0 %collective-permute-start = (bf16[128,512]{1,0:T(8,128)(2,1)S(1)}, bf16[128,512]{1,0:T(8,128)(2,1)S(1)}, u32[]{:S(2)}, u32[]{:S(2)}) collective-permute-start(bf16[128,512]{1,0:T(8,128)(2,1)S(1)} %get-tuple-element.32), channel_id=1, source_target_pairs={{0,1},{1,0},{2,3},{3,2},{4,5},{5,4},{6,7},{7,6},{8,9},{9,8},{10,11... | collective-permute-start | bytes 393224 | tf_op jit(solution)/shard_map/ppermute | solution.py:31
where the time goes:
time: 40.3 us; the launch traced here: 40.1 us
  starting transfers between devices  17.1 us (42%)
  Pallas kernels  13.8 us (34%)
  waiting for transfers between devices  7.1 us (18%)
  between operations  2.07 us (5%)
    ppermute x10, starting transfers between devices, swap(): return lax.ppermute(block, axis, route)  17.1 us
    pallas_call x13, Pallas kernels, call(): pl.pallas_call(body, name=getattr(body, 'func', body).__name__, out_shape...  13.8 us
    ppermute x10, waiting for transfers between devices, swap(): return lax.ppermute(block, axis, route)  7.1 us
  transfers between devices with their start and end apart: 10, of which 5 were waited for; matrix products, arithmetic and copies ran while one was open for 0% of the time, Pallas kernels for 26%

commit v1 on v0

--- a/solution.py
+++ b/solution.py
@@ -61,12 +61,12 @@
     return coeffs.astype(F32).T.astype(BF16)
 
 
-def is_owner(meta_ref):
-    return jnp.max(meta_ref[0:1, :]) > 0
-
-
-def alive_rows(meta_ref, shape, first=0):
-    return lax.broadcasted_iota(I32, shape, 0) + first < jnp.max(meta_ref[1:2, :])
+def is_owner(slot_ref):
+    return slot_ref[0] == lax.axis_index("grp")
+
+
+def alive_rows(count_ref, shape, first=0):
+    return lax.broadcasted_iota(I32, shape, 0) + first < count_ref[0]
 
 
 def own_half(group, half):
@@ -74,7 +74,7 @@
 
 
 def first_body(slot_ref, skel_ref, coeffs_ref, cross_ref, diag_ref, samples_ref, tests_ref,
-               message_ref, hot_ref, diag_rows_ref, meta_ref, cross_out_ref,
+               message_ref, hot_ref, diag_rows_ref, cross_out_ref,
                skel_buf, coeffs_buf, diag_buf, samples_buf, tests_buf, sems):
     group = lax.axis_index("grp")
     half = coeffs_ref.shape[0]
@@ -84,8 +84,7 @@
     copies = [pltpu.make_async_copy(src, dst, sems.at[i]) for i, (src, dst) in enumerate(pairs)]
     for copy in copies:
         copy.start()
-    owner = slot_ref[0] == group
-    meta_ref[...] = jnp.zeros(meta_ref.shape, I32) + jnp.where(owner, 1, 0)
+    owner = is_owner(slot_ref)
     copies[0].wait()
     hot = hot_rows(skel_buf[...], 2 * half)
     hot_ref[...] = hot
@@ -116,16 +115,14 @@
             mm(mine, samples_ref[:, cut]) + mm(diag_rows_ref[...], tests_ref[:, cut])).astype(BF16)
 
 
-def next_body(owner_ref, count_ref, coeffs_ref, hot_ref, diag_rows_ref, samples_ref, tests_ref,
-              own_ref, second_ref, partial_ref, slots_ref, meta_ref, coeffs_buf, sem):
+def next_body(slot_ref, count_ref, coeffs_ref, hot_ref, diag_rows_ref, samples_ref, tests_ref,
+              own_ref, second_ref, partial_ref, slots_ref, coeffs_buf, sem):
     group = lax.axis_index("grp")
     half = coeffs_ref.shape[0]
     width = own_ref.shape[1]
     copy = pltpu.make_async_copy(coeffs_ref, coeffs_buf, sem)
     copy.start()
-    owner = is_owner(owner_ref)
-    meta_ref[0:1, :] = owner_ref[0:1, :]
-    meta_ref[1:2, :] = jnp.zeros((1, 128), I32) + count_ref[0]
+    owner = is_owner(slot_ref)
     skel_rows(group, second_ref, width, hot_ref, diag_rows_ref, samples_ref, tests_ref)
     copy.wait()
 
@@ -142,29 +139,29 @@
             partial_ref[:, cut] = mm(slots, tests_ref[own_half(group, half), cut]) + mm(hot_ref[...], tests_ref[:, cut])
 
 
-def rest_body(meta_ref, slots_ref, hot_ref, diag_rows_ref, samples_ref, tests_ref, *outs):
+def rest_body(slot_ref, slots_ref, hot_ref, diag_rows_ref, samples_ref, tests_ref, *outs):
     group = lax.axis_index("grp")
     others_ref = outs[-1]
     share = others_ref.shape[0]
     for i, out_ref in enumerate(outs[:-1]):
         skel_rows(group, out_ref, (i + 2) * out_ref.shape[1], hot_ref, diag_rows_ref, samples_ref, tests_ref)
 
-    @pl.when(is_owner(meta_ref))
+    @pl.when(is_owner(slot_ref))
     def _():
         others_ref[...] = jnp.zeros(others_ref.shape, BF16)
 
-    @pl.when(jnp.logical_not(is_owner(meta_ref)))
+    @pl.when(jnp.logical_not(is_owner(slot_ref)))
     def _():
         others_ref[...] = slots_ref[own_half(1 - group, share), :]
 
 
-def send_body(index, meta_ref, first_got_ref, own_ref, got_ref, partial_ref, slots_ref, hot_ref, tests_ref, *rest):
+def send_body(index, slot_ref, count_ref, first_got_ref, own_ref, got_ref, partial_ref, slots_ref, hot_ref, tests_ref, *rest):
     out_ref = rest[-1]
     group = lax.axis_index("grp")
     cap, width = out_ref.shape
     half = tests_ref.shape[0] // 2
-    owner = is_owner(meta_ref)
-    alive = alive_rows(meta_ref, (cap, BLOCK))
+    owner = is_owner(slot_ref)
+    alive = alive_rows(count_ref, (cap, BLOCK))
 
     @pl.when(owner)
     def _():
@@ -187,12 +184,12 @@
             out_ref[:, at:at + BLOCK] = jnp.where(alive, part, 0.0).astype(BF16)
 
 
-def early_body(meta_ref, hot_ref, message_ref, slots_ref, tests_ref, share_ref, partial_ref):
+def early_body(slot_ref, hot_ref, message_ref, slots_ref, tests_ref, share_ref, partial_ref):
     group = lax.axis_index("grp")
     share, cols = share_ref.shape
     half = tests_ref.shape[0] // 2
     first = cols - partial_ref.shape[1]
-    owner = is_owner(meta_ref)
+    owner = is_owner(slot_ref)
     rows = own_half(group, share)
 
     @pl.when(owner)
@@ -210,7 +207,7 @@
                 mm(slots_ref[...], tests_ref[own_half(group, half), cut]) + mm(hot_ref[...], tests_ref[:, cut]))
 
 
-def generator_body(meta_ref, share_ref, others_ref, tests_ref, *rest):
+def generator_body(slot_ref, count_ref, share_ref, others_ref, tests_ref, *rest):
     sent = rest[:CHUNKS]
     out_ref, token_ref, buf, sems = rest[CHUNKS + 1:]
     token_ref[...] = jnp.zeros(token_ref.shape, I32)
@@ -218,14 +215,14 @@
     share, cols = out_ref.shape
     half = tests_ref.shape[0] // 2
     width = cols // CHUNKS
-    owner = is_owner(meta_ref)
+    owner = is_owner(slot_ref)
     rows = own_half(group, share)
     copies = [pltpu.make_async_copy(buf.at[:, pl.ds(i * width, width)], out_ref.at[:, pl.ds(i * width, width)], sems.at[i])
               for i in range(CHUNKS)]
 
     @pl.when(owner)
     def _():
-        alive = alive_rows(meta_ref, (share, BLOCK), group * share)
+        alive = alive_rows(count_ref, (share, BLOCK), group * share)
         for i in range(CHUNKS):
             for at in range(i * width, (i + 1) * width, BLOCK):
                 cut = slice(at, at + BLOCK)
@@ -243,13 +240,13 @@
         copy.wait()
 
 
-def parent_body(index, token, meta_ref, cross_ref, cross_got_ref, sent_ref, got_ref, *rest):
+def parent_body(index, token, slot_ref, cross_ref, cross_got_ref, sent_ref, got_ref, *rest):
     out_ref = rest[-3 - token]
     buf, sems = rest[-2:]
     if token:
         rest[-3][...] = jnp.zeros(rest[-3].shape, I32)
     width = sent_ref.shape[1]
-    owner = is_owner(meta_ref)
+    owner = is_owner(slot_ref)
     copies = [pltpu.make_async_copy(buf.at[:, pl.ds(at, BLOCK)], out_ref.at[:, pl.ds(index * width + at, BLOCK)],
                                     sems.at[at // BLOCK]) for at in range(0, width, BLOCK)]
 
@@ -283,11 +280,11 @@
         for x in (diag_block, coeffs, cross, skeleton, samples, test_matrix))
     piece = like((cap, width), BF16)
 
-    message, hot, diag_rows, owner, cross_near = call(
+    message, hot, diag_rows, cross_near = call(
         first_body,
-        (piece, like((cap, rows), BF16), like((cap, rows), BF16), like((8, 128), I32), like((cap, cap), BF16)),
+        (piece, like((cap, rows), BF16), like((cap, rows), BF16), like((cap, cap), BF16)),
         [SMEM] + [HBM] * 6,
-        (VMEM,) * 5,
+        (VMEM,) * 4,
         (parent_slot, skeleton_far, coeffs_far, cross_far, diag_far, samples_far, tests_far),
         [pltpu.VMEM((1, cap), I32), pltpu.VMEM((half, cap), BF16), pltpu.VMEM((half, rows), BF16),
          pltpu.VMEM((half, width), BF16), pltpu.VMEM((rows, width), BF16), dma((6,))],
@@ -295,12 +292,12 @@
     )
     got = [swap(message, "grp", 0)]
     cross_got = swap(cross_near, "node", SIB_BIT)
-    own0, own1, partial, slots, meta = call(
+    own0, own1, partial, slots = call(
         next_body,
-        (piece, piece, like((cap, width), F32), like((cap, half), BF16), like((8, 128), I32)),
-        [VMEM, SMEM, HBM] + [VMEM] * 4,
-        (VMEM,) * 5,
-        (owner, counts, coeffs_far, hot, diag_rows, samples, test_matrix),
+        (piece, piece, like((cap, width), F32), like((cap, half), BF16)),
+        [SMEM, SMEM, HBM] + [VMEM] * 4,
+        (VMEM,) * 4,
+        (parent_slot, counts, coeffs_far, hot, diag_rows, samples, test_matrix),
         [pltpu.VMEM((half, cap), BF16), dma],
         flops=4 * cap * (rows + half) * width, moved=2 * (half + rows) * width,
     )
@@ -308,17 +305,17 @@
     early, ready = call(
         early_body,
         (like((share, cols), F32), like((cap, READY * width), F32)),
-        [VMEM] * 5,
+        [SMEM] + [VMEM] * 4,
         (VMEM, VMEM),
-        (meta, hot, message, slots, test_matrix),
+        (parent_slot, hot, message, slots, test_matrix),
         flops=3 * share * rows * cols, moved=0,
     )
     *own, others = call(
         rest_body,
         (piece,) * (CHUNKS - 2) + (like((share, half), BF16),),
-        [VMEM] * 6,
+        [SMEM] + [VMEM] * 5,
         (VMEM,) * (CHUNKS - 1),
-        (meta, slots, hot, diag_rows, samples, test_matrix),
+        (parent_slot, slots, hot, diag_rows, samples, test_matrix),
         flops=2 * cap * (rows + half) * width * (CHUNKS - 2), moved=2 * half * width,
     )
     own = [own0, own1] + own
@@ -328,13 +325,13 @@
     sents = []
     tokens = []
     for i in range(CHUNKS):
-        hold = (tokens[i - 2],) if i >= 2 else (cross_got,) if i == 1 else (ready,)
+        hold = (tokens[i - 2],) if i >= 2 else (cross_got,) if i == 1 else (ready, cross_got)
         sent = call(
             functools.partial(send_body, i),
             piece,
-            [VMEM] * 8 + [ANY] * len(hold),
+            [SMEM] * 2 + [VMEM] * 7 + [ANY] * len(hold),
             VMEM,
-            (meta, got[0], own[i], got[i], ready if i >= CHUNKS - READY else partial, slots, hot, test_matrix) + hold,
+            (parent_slot, counts, got[0], own[i], got[i], ready if i >= CHUNKS - READY else partial, slots, hot, test_matrix) + hold,
             flops=2 * cap * half * width * (1 if i == 0 else 4), moved=4 * cap * width,
         )
         sents.append(sent)
@@ -343,20 +340,20 @@
             generators, token = call(
                 generator_body,
                 (like((share, cols), BF16), like((8, 128), I32)),
-                [VMEM] * (4 + CHUNKS) + [ANY],
+                [SMEM] * 2 + [VMEM] * (3 + CHUNKS) + [ANY],
                 (HBM, VMEM),
-                (meta, early, others_got, test_matrix, *sents, tokens[-1]),
+                (parent_slot, counts, early, others_got, test_matrix, *sents, tokens[-1]),
                 [pltpu.VMEM((share, cols), BF16), dma((CHUNKS,))],
-                flops=4 * share * rows * cols, moved=2 * (rows + share) * cols,
+                flops=32 * share * rows * cols, moved=16 * (rows + share) * cols,
             )
             tokens.append(token)
         token = i < CHUNKS - 1
         out, *more = call(
             functools.partial(parent_body, i, token),
             [like((cap, cols), F32)] + [like((8, 128), I32)] * token,
-            [VMEM] * 5 + ([] if out is None else [HBM]) + [ANY] * (not token),
+            [SMEM] + [VMEM] * 4 + ([] if out is None else [HBM]) + [ANY] * (not token),
             [HBM] + [VMEM] * token,
-            (meta, cross_near, cross_got, sent, arrived) + (() if out is None else (out,)) + tuple(tokens[-1:] * (not token)),
+            (parent_slot, cross_near, cross_got, sent, arrived) + (() if out is None else (out,)) + tuple(tokens[-1:] * (not token)),
             [pltpu.VMEM((cap, width), F32), dma((width // BLOCK,))],
             flops=2 * cap * cap * width, moved=8 * cap * width,
             alias=None if out is None else {5: 0},

time: 40.3 us -> 39.5 us (0.980)
  Pallas kernels: 13.8 us -> 11.5 us
  waiting for transfers between devices: 7.1 us -> 8.96 us
    pallas_call x13, Pallas kernels: 13.8 us -> 11.5 us  [call(): pl.pallas_call(body, name=getattr(body, 'func', body).__name__, out_shape...]
    ppermute x10, waiting for transfers between devices: 7.1 us -> 8.96 us  [swap(): return lax.ppermute(block, axis, route)]
  transfers between devices with their start and end apart: 10 -> 10, of which waited for: 5 -> 5; matrix products, arithmetic and copies ran while one was open for 0% -> 0% of each run, Pallas kernels for 26% -> 21%
where the time goes in v1:
time: 39.5 us; the launch traced here: 39.4 us
  starting transfers between devices  16.8 us (43%)
  Pallas kernels  11.5 us (29%)
  waiting for transfers between devices  8.96 us (23%)
  between operations  2.08 us (5%)
    ppermute x10, starting transfers between devices, swap(): return lax.ppermute(block, axis, route)  16.8 us
    pallas_call x13, Pallas kernels, call(): pl.pallas_call(body, name=getattr(body, 'func', body).__name__, out_shape...  11.5 us
    ppermute x10, waiting for transfers between devices, swap(): return lax.ppermute(block, axis, route)  8.96 us
  transfers between devices with their start and end apart: 10, of which 5 were waited for; matrix products, arithmetic and copies ran while one was open for 0% of the time, Pallas kernels for 21%

profile of v1, /device:TPU:0, one launch (start us, length us, event | category | flops | bytes accessed | tf_op | source)
XLA Modules:
  0.0 39.4 jit_solution(6746374530808011938)
XLA Ops:
  1.3 0.0 copy-start
  1.3 0.0 copy-start.1
  1.3 2.1 %first_body.1 = (bf16[256,512]{1,0:T(8,128)(2,1)S(1)}, bf16[256,1024]{1,0:T(8,128)(2,1)S(1)}, bf16[256,1024]{1,0:T(8,128)(2,1)S(1)}, bf16[256,256]{1,0:T(8,128)(2,1)S(1)}) custom-call(s32[1]{0:T(128)S(6)} %copy.17.slot_ref, s32[1,256]{1,0:T(1,128)} %skel_ref.1, bf16[512,256]{1,0:T(8,128)(2,1)} %coeffs_ref.3, bf16[256,256]{1,0:T(8,128)(2,1)} %cross_ref.1, ...), custom_call_target="tpu_custom_call" | custom-call | flops 536870912 | bytes 2621440 | tf_op jit(solution)/shard_map/first_body/pallas_call | solution.py:35
  3.5 3.5 %collective-permute-start.1 = (bf16[256,512]{1,0:T(8,128)(2,1)S(1)}, bf16[256,512]{1,0:T(8,128)(2,1)S(1)}, u32[]{:S(2)}, u32[]{:S(2)}) collective-permute-start(bf16[256,512]{1,0:T(8,128)(2,1)S(1)} %get-tuple-element.24.message_ref), channel_id=1, source_target_pairs={{0,1},{1,0},{2,3},{3,2},{4,5},{5,4},{6,7},{7,6},{8,9},{9,8},{10,11... | collective-permute-start | bytes 786440 | tf_op jit(solution)/shard_map/ppermute | solution.py:31
  6.9 1.1 %collective-permute-start.2 = (bf16[256,256]{1,0:T(8,128)(2,1)S(1)}, bf16[256,256]{1,0:T(8,128)(2,1)S(1)}, u32[]{:S(2)}, u32[]{:S(2)}) collective-permute-start(bf16[256,256]{1,0:T(8,128)(2,1)S(1)} %get-tuple-element.32.cross_ref), channel_id=1, source_target_pairs={{0,8},{8,0},{2,10},{10,2},{4,12},{12,4},{6,14},{14,6},{16,24},{24,... | collective-permute-start | bytes 393224 | tf_op jit(solution)/shard_map/ppermute | solution.py:31
  8.7 0.0 copy-done
  8.7 0.0 copy-done.1
  8.7 1.5 %next_body.1 = (bf16[256,512]{1,0:T(8,128)(2,1)S(1)}, bf16[256,512]{1,0:T(8,128)(2,1)S(1)}, f32[256,512]{1,0:T(8,128)S(1)}, bf16[256,512]{1,0:T(8,128)(2,1)S(1)}) custom-call(s32[1]{0:T(128)S(6)} %copy.17.slot_ref, s32[1]{0:T(128)S(6)} %copy.16.count_ref, bf16[512,256]{1,0:T(8,128)(2,1)} %coeffs_ref.3, bf16[256,1024]{1,0:T(8,128)(2,1)S(1)} %get-tuple-element.23.hot_ref, ...), custom_call_target="tpu_custom_call" | custom-call | flops 805306368 | bytes 1572864 | tf_op jit(solution)/shard_map/next_body/pallas_call | solution.py:35
  10.3 1.0 %collective-permute-start.3 = (bf16[256,512]{1,0:T(8,128)(2,1)S(1)}, bf16[256,512]{1,0:T(8,128)(2,1)S(1)}, u32[]{:S(2)}, u32[]{:S(2)}) collective-permute-start(bf16[256,512]{1,0:T(8,128)(2,1)S(1)} %get-tuple-element.33.own_ref), channel_id=1, source_target_pairs={{0,1},{1,0},{2,3},{3,2},{4,5},{5,4},{6,7},{7,6},{8,9},{9,8},{10,11... | collective-permute-start | bytes 786440 | tf_op jit(solution)/shard_map/ppermute | solution.py:31
  11.3 1.0 %early_body.1 = (f32[128,2048]{1,0:T(8,128)S(1)}, f32[256,1024]{1,0:T(8,128)S(1)}) custom-call(s32[1]{0:T(128)S(6)} %copy.17.slot_ref, bf16[256,1024]{1,0:T(8,128)(2,1)S(1)} %get-tuple-element.23.hot_ref, bf16[256,512]{1,0:T(8,128)(2,1)S(1)} %get-tuple-element.24.message_ref, bf16[256,512]{1,0:T(8,128)(2,1)S(1)} %get-tuple-element.26.slots_ref, ...), custom_call_target="tpu_custom_call" | custom-call | flops 805306368 | tf_op jit(solution)/shard_map/early_body/pallas_call | solution.py:35
  12.3 0.0 collective-permute-done.2.rest_1_.rest_0_.cross_got_ref
  12.3 1.8 %collective-permute-done.1.first_got_ref.got_ref = bf16[256,512]{1,0:T(8,128)(2,1)S(1)} collective-permute-done((bf16[256,512]{1,0:T(8,128)(2,1)S(1)}, bf16[256,512]{1,0:T(8,128)(2,1)S(1)}, u32[]{:S(2)}, u32[]{:S(2)}) %collective-permute-start.1) | collective-permute-done | bytes 262176 | tf_op jit(solution)/shard_map/ppermute | solution.py:31
  14.1 0.1 send_body.4.sent_ref.rest_0_
  14.2 2.4 %collective-permute-start.5 = (bf16[256,512]{1,0:T(8,128)(2,1)S(1)}, bf16[256,512]{1,0:T(8,128)(2,1)S(1)}, u32[]{:S(2)}, u32[]{:S(2)}) collective-permute-start(bf16[256,512]{1,0:T(8,128)(2,1)S(1)} %send_body.4.sent_ref.rest_0_), channel_id=1, source_target_pairs={{0,8},{8,0},{2,10},{10,2},{4,12},{12,4},{6,14},{14,6},{16,24},{24,... | collective-permute-start | bytes 786440 | tf_op jit(solution)/shard_map/ppermute | solution.py:31
  16.6 1.0 %rest_body.1 = (bf16[256,512]{1,0:T(8,128)(2,1)S(1)}, bf16[256,512]{1,0:T(8,128)(2,1)S(1)}, bf16[128,512]{1,0:T(8,128)(2,1)S(1)}) custom-call(s32[1]{0:T(128)S(6)} %copy.17.slot_ref, bf16[256,512]{1,0:T(8,128)(2,1)S(1)} %get-tuple-element.26.slots_ref, bf16[256,1024]{1,0:T(8,128)(2,1)S(1)} %get-tuple-element.23.hot_ref, ...), custom_call_target="tpu_custom_call" | custom-call | flops 805306368 | bytes 524288 | tf_op jit(solution)/shard_map/rest_body/pallas_call | solution.py:35
  17.5 0.9 %collective-permute-start.4 = (bf16[256,512]{1,0:T(8,128)(2,1)S(1)}, bf16[256,512]{1,0:T(8,128)(2,1)S(1)}, u32[]{:S(2)}, u32[]{:S(2)}) collective-permute-start(bf16[256,512]{1,0:T(8,128)(2,1)S(1)} %get-tuple-element.34.own_ref), channel_id=1, source_target_pairs={{0,1},{1,0},{2,3},{3,2},{4,5},{5,4},{6,7},{7,6},{8,9},{9,8},{10,11... | collective-permute-start | bytes 786440 | tf_op jit(solution)/shard_map/ppermute | solution.py:31
  18.5 1.2 %collective-permute-done.3.got_ref = bf16[256,512]{1,0:T(8,128)(2,1)S(1)} collective-permute-done((bf16[256,512]{1,0:T(8,128)(2,1)S(1)}, bf16[256,512]{1,0:T(8,128)(2,1)S(1)}, u32[]{:S(2)}, u32[]{:S(2)}) %collective-permute-start.3) | collective-permute-done | bytes 262176 | tf_op jit(solution)/shard_map/ppermute | solution.py:31
  19.7 0.1 send_body.5.sent_ref.rest_1_
  19.8 2.8 %collective-permute-start.7 = (bf16[256,512]{1,0:T(8,128)(2,1)S(1)}, bf16[256,512]{1,0:T(8,128)(2,1)S(1)}, u32[]{:S(2)}, u32[]{:S(2)}) collective-permute-start(bf16[256,512]{1,0:T(8,128)(2,1)S(1)} %send_body.5.sent_ref.rest_1_), channel_id=1, source_target_pairs={{0,8},{8,0},{2,10},{10,2},{4,12},{12,4},{6,14},{14,6},{16,24},{24,... | collective-permute-start | bytes 786440 | tf_op jit(solution)/shard_map/ppermute | solution.py:31
  22.6 0.5 %collective-permute-start.6 = (bf16[256,512]{1,0:T(8,128)(2,1)S(1)}, bf16[256,512]{1,0:T(8,128)(2,1)S(1)}, u32[]{:S(2)}, u32[]{:S(2)}) collective-permute-start(bf16[256,512]{1,0:T(8,128)(2,1)S(1)} %get-tuple-element.36.own_ref), channel_id=1, source_target_pairs={{0,1},{1,0},{2,3},{3,2},{4,5},{5,4},{6,7},{7,6},{8,9},{9,8},{10,11... | collective-permute-start | bytes 786440 | tf_op jit(solution)/shard_map/ppermute | solution.py:31
  23.0 0.0 collective-permute-done.5.got_ref
  23.0 1.1 %parent_body.4 = (f32[256,2048]{1,0:T(8,128)}, s32[8,128]{1,0:T(8,128)S(1)}) custom-call(s32[1]{0:T(128)S(6)} %copy.17.slot_ref, bf16[256,256]{1,0:T(8,128)(2,1)S(1)} %get-tuple-element.32.cross_ref, bf16[256,256]{1,0:T(8,128)(2,1)S(1)} %collective-permute-done.2.rest_1_.rest_0_.cross_got_ref, bf16[256,512]{1,0:T(8,128)(2,1)S(1)} %send_body.4.sent_ref.rest_0_, ...), custom_call_target="tpu_custom_call" | custom-call | flops 67108864 | bytes 1048576 | tf_op jit(solution)/shard_map/parent_body/pallas_call | solution.py:35
  24.1 2.0 %collective-permute-done.4.got_ref = bf16[256,512]{1,0:T(8,128)(2,1)S(1)} collective-permute-done((bf16[256,512]{1,0:T(8,128)(2,1)S(1)}, bf16[256,512]{1,0:T(8,128)(2,1)S(1)}, u32[]{:S(2)}, u32[]{:S(2)}) %collective-permute-start.4) | collective-permute-done | bytes 262176 | tf_op jit(solution)/shard_map/ppermute | solution.py:31
  26.1 0.1 send_body.6.sent_ref.rest_2_
  26.2 1.5 %collective-permute-start.8 = (bf16[256,512]{1,0:T(8,128)(2,1)S(1)}, bf16[256,512]{1,0:T(8,128)(2,1)S(1)}, u32[]{:S(2)}, u32[]{:S(2)}) collective-permute-start(bf16[256,512]{1,0:T(8,128)(2,1)S(1)} %send_body.6.sent_ref.rest_2_), channel_id=1, source_target_pairs={{0,8},{8,0},{2,10},{10,2},{4,12},{12,4},{6,14},{14,6},{16,24},{24,... | collective-permute-start | bytes 786440 | tf_op jit(solution)/shard_map/ppermute | solution.py:31
  27.8 1.2 %collective-permute-start = (bf16[128,512]{1,0:T(8,128)(2,1)S(1)}, bf16[128,512]{1,0:T(8,128)(2,1)S(1)}, u32[]{:S(2)}, u32[]{:S(2)}) collective-permute-start(bf16[128,512]{1,0:T(8,128)(2,1)S(1)} %get-tuple-element.28), channel_id=1, source_target_pairs={{0,1},{1,0},{2,3},{3,2},{4,5},{5,4},{6,7},{7,6},{8,9},{9,8},{10,11... | collective-permute-start | bytes 393224 | tf_op jit(solution)/shard_map/ppermute | solution.py:31
  29.0 0.0 collective-permute-done.7.got_ref
  29.0 1.1 %parent_body.5 = (f32[256,2048]{1,0:T(8,128)}, s32[8,128]{1,0:T(8,128)S(1)}) custom-call(s32[1]{0:T(128)S(6)} %copy.17.slot_ref, bf16[256,256]{1,0:T(8,128)(2,1)S(1)} %get-tuple-element.32.cross_ref, bf16[256,256]{1,0:T(8,128)(2,1)S(1)} %collective-permute-done.2.rest_1_.rest_0_.cross_got_ref, ...), custom_call_target="tpu_custom_call", output_to_operand_aliasing={{0}: (5, {})} | custom-call | flops 67108864 | bytes 1048576 | tf_op jit(solution)/shard_map/parent_body/pallas_call | solution.py:35
  30.1 1.4 %collective-permute-done.6.got_ref = bf16[256,512]{1,0:T(8,128)(2,1)S(1)} collective-permute-done((bf16[256,512]{1,0:T(8,128)(2,1)S(1)}, bf16[256,512]{1,0:T(8,128)(2,1)S(1)}, u32[]{:S(2)}, u32[]{:S(2)}) %collective-permute-start.6) | collective-permute-done | bytes 262176 | tf_op jit(solution)/shard_map/ppermute | solution.py:31
  31.5 0.1 send_body.7.rest_3_.sent_ref
  31.6 1.8 %collective-permute-start.9 = (bf16[256,512]{1,0:T(8,128)(2,1)S(1)}, bf16[256,512]{1,0:T(8,128)(2,1)S(1)}, u32[]{:S(2)}, u32[]{:S(2)}) collective-permute-start(bf16[256,512]{1,0:T(8,128)(2,1)S(1)} %send_body.7.rest_3_.sent_ref), channel_id=1, source_target_pairs={{0,8},{8,0},{2,10},{10,2},{4,12},{12,4},{6,14},{14,6},{16,24},{24,... | collective-permute-start | bytes 786440 | tf_op jit(solution)/shard_map/ppermute | solution.py:31
  33.4 0.0 collective-permute-done.8.got_ref
  33.4 1.1 %parent_body.6 = (f32[256,2048]{1,0:T(8,128)}, s32[8,128]{1,0:T(8,128)S(1)}) custom-call(s32[1]{0:T(128)S(6)} %copy.17.slot_ref, bf16[256,256]{1,0:T(8,128)(2,1)S(1)} %get-tuple-element.32.cross_ref, bf16[256,256]{1,0:T(8,128)(2,1)S(1)} %collective-permute-done.2.rest_1_.rest_0_.cross_got_ref, ...), custom_call_target="tpu_custom_call", output_to_operand_aliasing={{0}: (5, {})} | custom-call | flops 67108864 | bytes 1048576 | tf_op jit(solution)/shard_map/parent_body/pallas_call | solution.py:35
  34.5 0.0 collective-permute-done.others_ref
  34.5 1.2 %generator_body.1 = (bf16[128,2048]{1,0:T(8,128)(2,1)}, s32[8,128]{1,0:T(8,128)S(1)}) custom-call(s32[1]{0:T(128)S(6)} %copy.17.slot_ref, s32[1]{0:T(128)S(6)} %copy.16.count_ref, f32[128,2048]{1,0:T(8,128)S(1)} %get-tuple-element.27.share_ref, bf16[128,512]{1,0:T(8,128)(2,1)S(1)} %collective-permute-done.others_ref, bf16[1024,2048]{1,0:T(8,128)(2,1)S(1)} %copy-done, ...), custom_call_target="tpu_custom_call" | custom-call | flops 8589934592 | bytes 37748736 | tf_op jit(solution)/shard_map/generator_body/pallas_call | solution.py:35
  35.7 2.6 %collective-permute-done.9.got_ref = bf16[256,512]{1,0:T(8,128)(2,1)S(1)} collective-permute-done((bf16[256,512]{1,0:T(8,128)(2,1)S(1)}, bf16[256,512]{1,0:T(8,128)(2,1)S(1)}, u32[]{:S(2)}, u32[]{:S(2)}) %collective-permute-start.9) | collective-permute-done | bytes 262176 | tf_op jit(solution)/shard_map/ppermute | solution.py:31
  38.3 1.1 %parent_body.7 = f32[256,2048]{1,0:T(8,128)} custom-call(s32[1]{0:T(128)S(6)} %copy.17.slot_ref, bf16[256,256]{1,0:T(8,128)(2,1)S(1)} %get-tuple-element.32.cross_ref, bf16[256,256]{1,0:T(8,128)(2,1)S(1)} %collective-permute-done.2.rest_1_.rest_0_.cross_got_ref, bf16[256,512]{1,0:T(8,128)(2,1)S(1)} %send_body.7.rest_3_.sent_ref, ...), custom_call_target="tpu_custom_call", output_to_operand_aliasing={{}: (5, {})} | custom-call | flops 67108864 | bytes 1048576 | tf_op jit(solution)/shard_map/parent_body/pallas_call | solution.py:35
Async XLA Ops:
  1.3 7.4 %copy-start = (bf16[1024,2048]{1,0:T(8,128)(2,1)S(1)}, bf16[1024,2048]{1,0:T(8,128)(2,1)}, u32[]{:S(2)}) copy-start(bf16[1024,2048]{1,0:T(8,128)(2,1)} %tests_ref.17) | copy-start | bytes 12582916
  1.3 7.4 %copy-start.1 = (bf16[512,2048]{1,0:T(8,128)(2,1)S(1)}, bf16[512,2048]{1,0:T(8,128)(2,1)}, u32[]{:S(2)}) copy-start(bf16[512,2048]{1,0:T(8,128)(2,1)} %samples_ref.5) | copy-start | bytes 6291460
  3.5 10.6 %collective-permute-start.1 = (bf16[256,512]{1,0:T(8,128)(2,1)S(1)}, bf16[256,512]{1,0:T(8,128)(2,1)S(1)}, u32[]{:S(2)}, u32[]{:S(2)}) collective-permute-start(bf16[256,512]{1,0:T(8,128)(2,1)S(1)} %get-tuple-element.24.message_ref), channel_id=1, source_target_pairs={{0,1},{1,0},{2,3},{3,2},{4,5},{5,4},{6,7},{7,6},{8,9},{9,8},{10,11... | collective-permute-start | bytes 786440 | tf_op jit(solution)/shard_map/ppermute | solution.py:31
  6.9 5.4 %collective-permute-start.2 = (bf16[256,256]{1,0:T(8,128)(2,1)S(1)}, bf16[256,256]{1,0:T(8,128)(2,1)S(1)}, u32[]{:S(2)}, u32[]{:S(2)}) collective-permute-start(bf16[256,256]{1,0:T(8,128)(2,1)S(1)} %get-tuple-element.32.cross_ref), channel_id=1, source_target_pairs={{0,8},{8,0},{2,10},{10,2},{4,12},{12,4},{6,14},{14,6},{16,24},{24,... | collective-permute-start | bytes 393224 | tf_op jit(solution)/shard_map/ppermute | solution.py:31
  10.3 9.4 %collective-permute-start.3 = (bf16[256,512]{1,0:T(8,128)(2,1)S(1)}, bf16[256,512]{1,0:T(8,128)(2,1)S(1)}, u32[]{:S(2)}, u32[]{:S(2)}) collective-permute-start(bf16[256,512]{1,0:T(8,128)(2,1)S(1)} %get-tuple-element.33.own_ref), channel_id=1, source_target_pairs={{0,1},{1,0},{2,3},{3,2},{4,5},{5,4},{6,7},{7,6},{8,9},{9,8},{10,11... | collective-permute-start | bytes 786440 | tf_op jit(solution)/shard_map/ppermute | solution.py:31
  14.2 8.9 %collective-permute-start.5 = (bf16[256,512]{1,0:T(8,128)(2,1)S(1)}, bf16[256,512]{1,0:T(8,128)(2,1)S(1)}, u32[]{:S(2)}, u32[]{:S(2)}) collective-permute-start(bf16[256,512]{1,0:T(8,128)(2,1)S(1)} %send_body.4.sent_ref.rest_0_), channel_id=1, source_target_pairs={{0,8},{8,0},{2,10},{10,2},{4,12},{12,4},{6,14},{14,6},{16,24},{24,... | collective-permute-start | bytes 786440 | tf_op jit(solution)/shard_map/ppermute | solution.py:31
  17.5 8.6 %collective-permute-start.4 = (bf16[256,512]{1,0:T(8,128)(2,1)S(1)}, bf16[256,512]{1,0:T(8,128)(2,1)S(1)}, u32[]{:S(2)}, u32[]{:S(2)}) collective-permute-start(bf16[256,512]{1,0:T(8,128)(2,1)S(1)} %get-tuple-element.34.own_ref), channel_id=1, source_target_pairs={{0,1},{1,0},{2,3},{3,2},{4,5},{5,4},{6,7},{7,6},{8,9},{9,8},{10,11... | collective-permute-start | bytes 786440 | tf_op jit(solution)/shard_map/ppermute | solution.py:31
  19.8 9.2 %collective-permute-start.7 = (bf16[256,512]{1,0:T(8,128)(2,1)S(1)}, bf16[256,512]{1,0:T(8,128)(2,1)S(1)}, u32[]{:S(2)}, u32[]{:S(2)}) collective-permute-start(bf16[256,512]{1,0:T(8,128)(2,1)S(1)} %send_body.5.sent_ref.rest_1_), channel_id=1, source_target_pairs={{0,8},{8,0},{2,10},{10,2},{4,12},{12,4},{6,14},{14,6},{16,24},{24,... | collective-permute-start | bytes 786440 | tf_op jit(solution)/shard_map/ppermute | solution.py:31
  22.6 8.9 %collective-permute-start.6 = (bf16[256,512]{1,0:T(8,128)(2,1)S(1)}, bf16[256,512]{1,0:T(8,128)(2,1)S(1)}, u32[]{:S(2)}, u32[]{:S(2)}) collective-permute-start(bf16[256,512]{1,0:T(8,128)(2,1)S(1)} %get-tuple-element.36.own_ref), channel_id=1, source_target_pairs={{0,1},{1,0},{2,3},{3,2},{4,5},{5,4},{6,7},{7,6},{8,9},{9,8},{10,11... | collective-permute-start | bytes 786440 | tf_op jit(solution)/shard_map/ppermute | solution.py:31
  26.2 7.2 %collective-permute-start.8 = (bf16[256,512]{1,0:T(8,128)(2,1)S(1)}, bf16[256,512]{1,0:T(8,128)(2,1)S(1)}, u32[]{:S(2)}, u32[]{:S(2)}) collective-permute-start(bf16[256,512]{1,0:T(8,128)(2,1)S(1)} %send_body.6.sent_ref.rest_2_), channel_id=1, source_target_pairs={{0,8},{8,0},{2,10},{10,2},{4,12},{12,4},{6,14},{14,6},{16,24},{24,... | collective-permute-start | bytes 786440 | tf_op jit(solution)/shard_map/ppermute | solution.py:31
  27.8 6.7 %collective-permute-start = (bf16[128,512]{1,0:T(8,128)(2,1)S(1)}, bf16[128,512]{1,0:T(8,128)(2,1)S(1)}, u32[]{:S(2)}, u32[]{:S(2)}) collective-permute-start(bf16[128,512]{1,0:T(8,128)(2,1)S(1)} %get-tuple-element.28), channel_id=1, source_target_pairs={{0,1},{1,0},{2,3},{3,2},{4,5},{5,4},{6,7},{7,6},{8,9},{9,8},{10,11... | collective-permute-start | bytes 393224 | tf_op jit(solution)/shard_map/ppermute | solution.py:31
  31.6 6.7 %collective-permute-start.9 = (bf16[256,512]{1,0:T(8,128)(2,1)S(1)}, bf16[256,512]{1,0:T(8,128)(2,1)S(1)}, u32[]{:S(2)}, u32[]{:S(2)}) collective-permute-start(bf16[256,512]{1,0:T(8,128)(2,1)S(1)} %send_body.7.rest_3_.sent_ref), channel_id=1, source_target_pairs={{0,8},{8,0},{2,10},{10,2},{4,12},{12,4},{6,14},{14,6},{16,24},{24,... | collective-permute-start | bytes 786440 | tf_op jit(solution)/shard_map/ppermute | solution.py:31

commit v2 on v1

--- a/solution.py
+++ b/solution.py
@@ -139,11 +139,14 @@
             partial_ref[:, cut] = mm(slots, tests_ref[own_half(group, half), cut]) + mm(hot_ref[...], tests_ref[:, cut])
 
 
-def rest_body(slot_ref, slots_ref, hot_ref, diag_rows_ref, samples_ref, tests_ref, *outs):
-    group = lax.axis_index("grp")
-    others_ref = outs[-1]
+def rest_body(slot_ref, count_ref, slots_ref, hot_ref, diag_rows_ref, samples_ref, tests_ref, ready_ref, first_got_ref, *rest):
+    outs, others_ref, done_ref = rest[-CHUNKS:-2], rest[-2], rest[-1]
+    group = lax.axis_index("grp")
     share = others_ref.shape[0]
-    for i, out_ref in enumerate(outs[:-1]):
+    cap, width = done_ref.shape
+    half = tests_ref.shape[0] // 2
+    first = tests_ref.shape[1] - width
+    for i, out_ref in enumerate(outs):
         skel_rows(group, out_ref, (i + 2) * out_ref.shape[1], hot_ref, diag_rows_ref, samples_ref, tests_ref)
 
     @pl.when(is_owner(slot_ref))
@@ -153,6 +156,11 @@
     @pl.when(jnp.logical_not(is_owner(slot_ref)))
     def _():
         others_ref[...] = slots_ref[own_half(1 - group, share), :]
+        alive = alive_rows(count_ref, (cap, BLOCK))
+        for at in range(0, width, BLOCK):
+            part = ready_ref[:, at:at + BLOCK] + mm(
+                first_got_ref[...], tests_ref[own_half(1 - group, half), first + at:first + at + BLOCK])
+            done_ref[:, at:at + BLOCK] = jnp.where(alive, part, 0.0).astype(BF16)
 
 
 def send_body(index, slot_ref, count_ref, first_got_ref, own_ref, got_ref, partial_ref, slots_ref, hot_ref, tests_ref, *rest):
@@ -168,6 +176,14 @@
         for at in range(0, width, BLOCK):
             cut = slice(at, at + BLOCK)
             out_ref[:, cut] = jnp.where(alive, own_ref[:, cut].astype(F32) + got_ref[:, cut].astype(F32), DEAD).astype(BF16)
+
+    if index >= CHUNKS - READY:
+        @pl.when(jnp.logical_not(owner))
+        def _():
+            place = (index - CHUNKS + READY) * width
+            out_ref[...] = partial_ref[:, place:place + width]
+
+        return
 
     @pl.when(jnp.logical_not(owner))
     def _():
@@ -176,9 +192,6 @@
             part = mm(first_got_ref[...], tests_ref[own_half(1 - group, half), cut])
             if index == 0:
                 part += partial_ref[:, cut]
-            elif index >= CHUNKS - READY:
-                place = index * width + at - (CHUNKS - READY) * width
-                part += partial_ref[:, place:place + BLOCK]
             else:
                 part += mm(slots_ref[...], tests_ref[own_half(group, half), cut]) + mm(hot_ref[...], tests_ref[:, cut])
             out_ref[:, at:at + BLOCK] = jnp.where(alive, part, 0.0).astype(BF16)
@@ -310,12 +323,12 @@
         (parent_slot, hot, message, slots, test_matrix),
         flops=3 * share * rows * cols, moved=0,
     )
-    *own, others = call(
+    *own, others, done = call(
         rest_body,
-        (piece,) * (CHUNKS - 2) + (like((share, half), BF16),),
-        [SMEM] + [VMEM] * 5,
-        (VMEM,) * (CHUNKS - 1),
-        (parent_slot, slots, hot, diag_rows, samples, test_matrix),
+        (piece,) * (CHUNKS - 2) + (like((share, half), BF16), like((cap, READY * width), BF16)),
+        [SMEM] * 2 + [VMEM] * 7,
+        (VMEM,) * CHUNKS,
+        (parent_slot, counts, slots, hot, diag_rows, samples, test_matrix, ready, got[0]),
         flops=2 * cap * (rows + half) * width * (CHUNKS - 2), moved=2 * half * width,
     )
     own = [own0, own1] + own
@@ -331,7 +344,7 @@
             piece,
             [SMEM] * 2 + [VMEM] * 7 + [ANY] * len(hold),
             VMEM,
-            (parent_slot, counts, got[0], own[i], got[i], ready if i >= CHUNKS - READY else partial, slots, hot, test_matrix) + hold,
+            (parent_slot, counts, got[0], own[i], got[i], done if i >= CHUNKS - READY else partial, slots, hot, test_matrix) + hold,
             flops=2 * cap * half * width * (1 if i == 0 else 4), moved=4 * cap * width,
         )
         sents.append(sent)

time: 39.5 us -> 39.2 us (level)
  transfers between devices with their start and end apart: 10 -> 10, of which waited for: 5 -> 6; matrix products, arithmetic and copies ran while one was open for 0% -> 0% of each run, Pallas kernels for 21% -> 21%
where the time goes in v2:
time: 39.2 us; the launch traced here: 39.4 us
  starting transfers between devices  17 us (43%)
  Pallas kernels  11.5 us (29%)
  waiting for transfers between devices  8.81 us (22%)
  between operations  2.08 us (5%)
    ppermute x10, starting transfers between devices, swap(): return lax.ppermute(block, axis, route)  17 us
    pallas_call x13, Pallas kernels, call(): pl.pallas_call(body, name=getattr(body, 'func', body).__name__, out_shape...  11.5 us
    ppermute x10, waiting for transfers between devices, swap(): return lax.ppermute(block, axis, route)  8.81 us
  transfers between devices with their start and end apart: 10, of which 6 were waited for; matrix products, arithmetic and copies ran while one was open for 0% of the time, Pallas kernels for 21%

profile of v2, /device:TPU:0, one launch (start us, length us, event | category | flops | bytes accessed | tf_op | source)
XLA Modules:
  0.0 39.4 jit_solution(10609177232775901008)
XLA Ops:
  1.3 0.0 copy-start
  1.3 0.0 copy-start.1
  1.3 2.1 %first_body.1 = (bf16[256,512]{1,0:T(8,128)(2,1)S(1)}, bf16[256,1024]{1,0:T(8,128)(2,1)S(1)}, bf16[256,1024]{1,0:T(8,128)(2,1)S(1)}, bf16[256,256]{1,0:T(8,128)(2,1)S(1)}) custom-call(s32[1]{0:T(128)S(6)} %copy.17.slot_ref, s32[1,256]{1,0:T(1,128)} %skel_ref.1, bf16[512,256]{1,0:T(8,128)(2,1)} %coeffs_ref.3, bf16[256,256]{1,0:T(8,128)(2,1)} %cross_ref.1, ...), custom_call_target="tpu_custom_call" | custom-call | flops 536870912 | bytes 2621440 | tf_op jit(solution)/shard_map/first_body/pallas_call | solution.py:35
  3.5 3.5 %collective-permute-start = (bf16[256,512]{1,0:T(8,128)(2,1)S(1)}, bf16[256,512]{1,0:T(8,128)(2,1)S(1)}, u32[]{:S(2)}, u32[]{:S(2)}) collective-permute-start(bf16[256,512]{1,0:T(8,128)(2,1)S(1)} %get-tuple-element.25.message_ref), channel_id=1, source_target_pairs={{0,1},{1,0},{2,3},{3,2},{4,5},{5,4},{6,7},{7,6},{8,9},{9,8},{10,11... | collective-permute-start | bytes 786440 | tf_op jit(solution)/shard_map/ppermute | solution.py:31
  6.9 1.1 %collective-permute-start.2 = (bf16[256,256]{1,0:T(8,128)(2,1)S(1)}, bf16[256,256]{1,0:T(8,128)(2,1)S(1)}, u32[]{:S(2)}, u32[]{:S(2)}) collective-permute-start(bf16[256,256]{1,0:T(8,128)(2,1)S(1)} %get-tuple-element.33.cross_ref), channel_id=1, source_target_pairs={{0,8},{8,0},{2,10},{10,2},{4,12},{12,4},{6,14},{14,6},{16,24},{24,... | collective-permute-start | bytes 393224 | tf_op jit(solution)/shard_map/ppermute | solution.py:31
  8.7 0.0 copy-done
  8.7 0.0 copy-done.1
  8.7 1.5 %next_body.1 = (bf16[256,512]{1,0:T(8,128)(2,1)S(1)}, bf16[256,512]{1,0:T(8,128)(2,1)S(1)}, f32[256,512]{1,0:T(8,128)S(1)}, bf16[256,512]{1,0:T(8,128)(2,1)S(1)}) custom-call(s32[1]{0:T(128)S(6)} %copy.17.slot_ref, s32[1]{0:T(128)S(6)} %copy.16.count_ref, bf16[512,256]{1,0:T(8,128)(2,1)} %coeffs_ref.3, bf16[256,1024]{1,0:T(8,128)(2,1)S(1)} %get-tuple-element.24.hot_ref, ...), custom_call_target="tpu_custom_call" | custom-call | flops 805306368 | bytes 1572864 | tf_op jit(solution)/shard_map/next_body/pallas_call | solution.py:35
  10.3 1.0 %collective-permute-start.3 = (bf16[256,512]{1,0:T(8,128)(2,1)S(1)}, bf16[256,512]{1,0:T(8,128)(2,1)S(1)}, u32[]{:S(2)}, u32[]{:S(2)}) collective-permute-start(bf16[256,512]{1,0:T(8,128)(2,1)S(1)} %get-tuple-element.34.own_ref), channel_id=1, source_target_pairs={{0,1},{1,0},{2,3},{3,2},{4,5},{5,4},{6,7},{7,6},{8,9},{9,8},{10,11... | collective-permute-start | bytes 786440 | tf_op jit(solution)/shard_map/ppermute | solution.py:31
  11.3 1.0 %early_body.1 = (f32[128,2048]{1,0:T(8,128)S(1)}, f32[256,1024]{1,0:T(8,128)S(1)}) custom-call(s32[1]{0:T(128)S(6)} %copy.17.slot_ref, bf16[256,1024]{1,0:T(8,128)(2,1)S(1)} %get-tuple-element.24.hot_ref, bf16[256,512]{1,0:T(8,128)(2,1)S(1)} %get-tuple-element.25.message_ref, bf16[256,512]{1,0:T(8,128)(2,1)S(1)} %get-tuple-element.27.slots_ref, ...), custom_call_target="tpu_custom_call" | custom-call | flops 805306368 | tf_op jit(solution)/shard_map/early_body/pallas_call | solution.py:35
  12.3 0.0 collective-permute-done.2.rest_1_.rest_0_.cross_got_ref
  12.3 1.8 %collective-permute-done.first_got_ref.got_ref = bf16[256,512]{1,0:T(8,128)(2,1)S(1)} collective-permute-done((bf16[256,512]{1,0:T(8,128)(2,1)S(1)}, bf16[256,512]{1,0:T(8,128)(2,1)S(1)}, u32[]{:S(2)}, u32[]{:S(2)}) %collective-permute-start) | collective-permute-done | bytes 262176 | tf_op jit(solution)/shard_map/ppermute | solution.py:31
  14.1 0.1 send_body.4.sent_ref.rest_0_
  14.2 2.4 %collective-permute-start.5 = (bf16[256,512]{1,0:T(8,128)(2,1)S(1)}, bf16[256,512]{1,0:T(8,128)(2,1)S(1)}, u32[]{:S(2)}, u32[]{:S(2)}) collective-permute-start(bf16[256,512]{1,0:T(8,128)(2,1)S(1)} %send_body.4.sent_ref.rest_0_), channel_id=1, source_target_pairs={{0,8},{8,0},{2,10},{10,2},{4,12},{12,4},{6,14},{14,6},{16,24},{24,... | collective-permute-start | bytes 786440 | tf_op jit(solution)/shard_map/ppermute | solution.py:31
  16.6 1.0 %rest_body.1 = (bf16[256,512]{1,0:T(8,128)(2,1)S(1)}, bf16[256,512]{1,0:T(8,128)(2,1)S(1)}, bf16[128,512]{1,0:T(8,128)(2,1)S(1)}, bf16[256,1024]{1,0:T(8,128)(2,1)S(1)}) custom-call(s32[1]{0:T(128)S(6)} %copy.17.slot_ref, s32[1]{0:T(128)S(6)} %copy.16.count_ref, bf16[256,512]{1,0:T(8,128)(2,1)S(1)} %get-tuple-element.27.slots_ref, ...), custom_call_target="tpu_custom_call" | custom-call | flops 805306368 | bytes 524288 | tf_op jit(solution)/shard_map/rest_body/pallas_call | solution.py:35
  17.5 1.4 %collective-permute-start.4 = (bf16[256,512]{1,0:T(8,128)(2,1)S(1)}, bf16[256,512]{1,0:T(8,128)(2,1)S(1)}, u32[]{:S(2)}, u32[]{:S(2)}) collective-permute-start(bf16[256,512]{1,0:T(8,128)(2,1)S(1)} %get-tuple-element.35.own_ref), channel_id=1, source_target_pairs={{0,1},{1,0},{2,3},{3,2},{4,5},{5,4},{6,7},{7,6},{8,9},{9,8},{10,11... | collective-permute-start | bytes 786440 | tf_op jit(solution)/shard_map/ppermute | solution.py:31
  18.9 0.7 %collective-permute-done.3.got_ref = bf16[256,512]{1,0:T(8,128)(2,1)S(1)} collective-permute-done((bf16[256,512]{1,0:T(8,128)(2,1)S(1)}, bf16[256,512]{1,0:T(8,128)(2,1)S(1)}, u32[]{:S(2)}, u32[]{:S(2)}) %collective-permute-start.3) | collective-permute-done | bytes 262176 | tf_op jit(solution)/shard_map/ppermute | solution.py:31
  19.7 0.1 send_body.5.sent_ref.rest_1_
  19.8 2.8 %collective-permute-start.7 = (bf16[256,512]{1,0:T(8,128)(2,1)S(1)}, bf16[256,512]{1,0:T(8,128)(2,1)S(1)}, u32[]{:S(2)}, u32[]{:S(2)}) collective-permute-start(bf16[256,512]{1,0:T(8,128)(2,1)S(1)} %send_body.5.sent_ref.rest_1_), channel_id=1, source_target_pairs={{0,8},{8,0},{2,10},{10,2},{4,12},{12,4},{6,14},{14,6},{16,24},{24,... | collective-permute-start | bytes 786440 | tf_op jit(solution)/shard_map/ppermute | solution.py:31
  22.6 0.5 %collective-permute-start.6 = (bf16[256,512]{1,0:T(8,128)(2,1)S(1)}, bf16[256,512]{1,0:T(8,128)(2,1)S(1)}, u32[]{:S(2)}, u32[]{:S(2)}) collective-permute-start(bf16[256,512]{1,0:T(8,128)(2,1)S(1)} %get-tuple-element.38.own_ref), channel_id=1, source_target_pairs={{0,1},{1,0},{2,3},{3,2},{4,5},{5,4},{6,7},{7,6},{8,9},{9,8},{10,11... | collective-permute-start | bytes 786440 | tf_op jit(solution)/shard_map/ppermute | solution.py:31
  23.0 0.0 collective-permute-done.5.got_ref
  23.0 1.1 %parent_body.4 = (f32[256,2048]{1,0:T(8,128)}, s32[8,128]{1,0:T(8,128)S(1)}) custom-call(s32[1]{0:T(128)S(6)} %copy.17.slot_ref, bf16[256,256]{1,0:T(8,128)(2,1)S(1)} %get-tuple-element.33.cross_ref, bf16[256,256]{1,0:T(8,128)(2,1)S(1)} %collective-permute-done.2.rest_1_.rest_0_.cross_got_ref, bf16[256,512]{1,0:T(8,128)(2,1)S(1)} %send_body.4.sent_ref.rest_0_, ...), custom_call_target="tpu_custom_call" | custom-call | flops 67108864 | bytes 1048576 | tf_op jit(solution)/shard_map/parent_body/pallas_call | solution.py:35
  24.1 2.0 %collective-permute-done.4.got_ref = bf16[256,512]{1,0:T(8,128)(2,1)S(1)} collective-permute-done((bf16[256,512]{1,0:T(8,128)(2,1)S(1)}, bf16[256,512]{1,0:T(8,128)(2,1)S(1)}, u32[]{:S(2)}, u32[]{:S(2)}) %collective-permute-start.4) | collective-permute-done | bytes 262176 | tf_op jit(solution)/shard_map/ppermute | solution.py:31
  26.1 0.1 send_body.6.sent_ref.rest_2_
  26.2 1.3 %collective-permute-start.8 = (bf16[256,512]{1,0:T(8,128)(2,1)S(1)}, bf16[256,512]{1,0:T(8,128)(2,1)S(1)}, u32[]{:S(2)}, u32[]{:S(2)}) collective-permute-start(bf16[256,512]{1,0:T(8,128)(2,1)S(1)} %send_body.6.sent_ref.rest_2_), channel_id=1, source_target_pairs={{0,8},{8,0},{2,10},{10,2},{4,12},{12,4},{6,14},{14,6},{16,24},{24,... | collective-permute-start | bytes 786440 | tf_op jit(solution)/shard_map/ppermute | solution.py:31
  27.5 1.5 %collective-permute-start.1 = (bf16[128,512]{1,0:T(8,128)(2,1)S(1)}, bf16[128,512]{1,0:T(8,128)(2,1)S(1)}, u32[]{:S(2)}, u32[]{:S(2)}) collective-permute-start(bf16[128,512]{1,0:T(8,128)(2,1)S(1)} %get-tuple-element.30), channel_id=1, source_target_pairs={{0,1},{1,0},{2,3},{3,2},{4,5},{5,4},{6,7},{7,6},{8,9},{9,8},{10,11... | collective-permute-start | bytes 393224 | tf_op jit(solution)/shard_map/ppermute | solution.py:31
  29.0 0.0 collective-permute-done.7.got_ref
  29.0 1.1 %parent_body.5 = (f32[256,2048]{1,0:T(8,128)}, s32[8,128]{1,0:T(8,128)S(1)}) custom-call(s32[1]{0:T(128)S(6)} %copy.17.slot_ref, bf16[256,256]{1,0:T(8,128)(2,1)S(1)} %get-tuple-element.33.cross_ref, bf16[256,256]{1,0:T(8,128)(2,1)S(1)} %collective-permute-done.2.rest_1_.rest_0_.cross_got_ref, ...), custom_call_target="tpu_custom_call", output_to_operand_aliasing={{0}: (5, {})} | custom-call | flops 67108864 | bytes 1048576 | tf_op jit(solution)/shard_map/parent_body/pallas_call | solution.py:35
  30.1 1.4 %collective-permute-done.6.got_ref = bf16[256,512]{1,0:T(8,128)(2,1)S(1)} collective-permute-done((bf16[256,512]{1,0:T(8,128)(2,1)S(1)}, bf16[256,512]{1,0:T(8,128)(2,1)S(1)}, u32[]{:S(2)}, u32[]{:S(2)}) %collective-permute-start.6) | collective-permute-done | bytes 262176 | tf_op jit(solution)/shard_map/ppermute | solution.py:31
  31.5 0.1 send_body.7.rest_3_.sent_ref
  31.6 1.5 %collective-permute-start.9 = (bf16[256,512]{1,0:T(8,128)(2,1)S(1)}, bf16[256,512]{1,0:T(8,128)(2,1)S(1)}, u32[]{:S(2)}, u32[]{:S(2)}) collective-permute-start(bf16[256,512]{1,0:T(8,128)(2,1)S(1)} %send_body.7.rest_3_.sent_ref), channel_id=1, source_target_pairs={{0,8},{8,0},{2,10},{10,2},{4,12},{12,4},{6,14},{14,6},{16,24},{24,... | collective-permute-start | bytes 786440 | tf_op jit(solution)/shard_map/ppermute | solution.py:31
  33.1 0.4 collective-permute-done.8.got_ref
  33.5 1.1 %parent_body.6 = (f32[256,2048]{1,0:T(8,128)}, s32[8,128]{1,0:T(8,128)S(1)}) custom-call(s32[1]{0:T(128)S(6)} %copy.17.slot_ref, bf16[256,256]{1,0:T(8,128)(2,1)S(1)} %get-tuple-element.33.cross_ref, bf16[256,256]{1,0:T(8,128)(2,1)S(1)} %collective-permute-done.2.rest_1_.rest_0_.cross_got_ref, ...), custom_call_target="tpu_custom_call", output_to_operand_aliasing={{0}: (5, {})} | custom-call | flops 67108864 | bytes 1048576 | tf_op jit(solution)/shard_map/parent_body/pallas_call | solution.py:35
  34.6 0.0 collective-permute-done.1.others_ref
  34.6 1.2 %generator_body.1 = (bf16[128,2048]{1,0:T(8,128)(2,1)}, s32[8,128]{1,0:T(8,128)S(1)}) custom-call(s32[1]{0:T(128)S(6)} %copy.17.slot_ref, s32[1]{0:T(128)S(6)} %copy.16.count_ref, f32[128,2048]{1,0:T(8,128)S(1)} %get-tuple-element.28.share_ref, bf16[128,512]{1,0:T(8,128)(2,1)S(1)} %collective-permute-done.1.others_ref, bf16[1024,2048]{1,0:T(8,128)(2,1)S(1)} %copy-done, ...), custom_call_target="tpu_custom_call" | custom-call | flops 8589934592 | bytes 37748736 | tf_op jit(solution)/shard_map/generator_body/pallas_call | solution.py:35
  35.8 2.5 %collective-permute-done.9.got_ref = bf16[256,512]{1,0:T(8,128)(2,1)S(1)} collective-permute-done((bf16[256,512]{1,0:T(8,128)(2,1)S(1)}, bf16[256,512]{1,0:T(8,128)(2,1)S(1)}, u32[]{:S(2)}, u32[]{:S(2)}) %collective-permute-start.9) | collective-permute-done | bytes 262176 | tf_op jit(solution)/shard_map/ppermute | solution.py:31
  38.3 1.1 %parent_body.7 = f32[256,2048]{1,0:T(8,128)} custom-call(s32[1]{0:T(128)S(6)} %copy.17.slot_ref, bf16[256,256]{1,0:T(8,128)(2,1)S(1)} %get-tuple-element.33.cross_ref, bf16[256,256]{1,0:T(8,128)(2,1)S(1)} %collective-permute-done.2.rest_1_.rest_0_.cross_got_ref, bf16[256,512]{1,0:T(8,128)(2,1)S(1)} %send_body.7.rest_3_.sent_ref, ...), custom_call_target="tpu_custom_call", output_to_operand_aliasing={{}: (5, {})} | custom-call | flops 67108864 | bytes 1048576 | tf_op jit(solution)/shard_map/parent_body/pallas_call | solution.py:35
Async XLA Ops:
  1.3 7.4 %copy-start = (bf16[1024,2048]{1,0:T(8,128)(2,1)S(1)}, bf16[1024,2048]{1,0:T(8,128)(2,1)}, u32[]{:S(2)}) copy-start(bf16[1024,2048]{1,0:T(8,128)(2,1)} %tests_ref.17) | copy-start | bytes 12582916
  1.3 7.4 %copy-start.1 = (bf16[512,2048]{1,0:T(8,128)(2,1)S(1)}, bf16[512,2048]{1,0:T(8,128)(2,1)}, u32[]{:S(2)}) copy-start(bf16[512,2048]{1,0:T(8,128)(2,1)} %samples_ref.5) | copy-start | bytes 6291460
  3.5 10.6 %collective-permute-start = (bf16[256,512]{1,0:T(8,128)(2,1)S(1)}, bf16[256,512]{1,0:T(8,128)(2,1)S(1)}, u32[]{:S(2)}, u32[]{:S(2)}) collective-permute-start(bf16[256,512]{1,0:T(8,128)(2,1)S(1)} %get-tuple-element.25.message_ref), channel_id=1, source_target_pairs={{0,1},{1,0},{2,3},{3,2},{4,5},{5,4},{6,7},{7,6},{8,9},{9,8},{10,11... | collective-permute-start | bytes 786440 | tf_op jit(solution)/shard_map/ppermute | solution.py:31
  6.9 5.4 %collective-permute-start.2 = (bf16[256,256]{1,0:T(8,128)(2,1)S(1)}, bf16[256,256]{1,0:T(8,128)(2,1)S(1)}, u32[]{:S(2)}, u32[]{:S(2)}) collective-permute-start(bf16[256,256]{1,0:T(8,128)(2,1)S(1)} %get-tuple-element.33.cross_ref), channel_id=1, source_target_pairs={{0,8},{8,0},{2,10},{10,2},{4,12},{12,4},{6,14},{14,6},{16,24},{24,... | collective-permute-start | bytes 393224 | tf_op jit(solution)/shard_map/ppermute | solution.py:31
  10.3 9.4 %collective-permute-start.3 = (bf16[256,512]{1,0:T(8,128)(2,1)S(1)}, bf16[256,512]{1,0:T(8,128)(2,1)S(1)}, u32[]{:S(2)}, u32[]{:S(2)}) collective-permute-start(bf16[256,512]{1,0:T(8,128)(2,1)S(1)} %get-tuple-element.34.own_ref), channel_id=1, source_target_pairs={{0,1},{1,0},{2,3},{3,2},{4,5},{5,4},{6,7},{7,6},{8,9},{9,8},{10,11... | collective-permute-start | bytes 786440 | tf_op jit(solution)/shard_map/ppermute | solution.py:31
  14.2 8.9 %collective-permute-start.5 = (bf16[256,512]{1,0:T(8,128)(2,1)S(1)}, bf16[256,512]{1,0:T(8,128)(2,1)S(1)}, u32[]{:S(2)}, u32[]{:S(2)}) collective-permute-start(bf16[256,512]{1,0:T(8,128)(2,1)S(1)} %send_body.4.sent_ref.rest_0_), channel_id=1, source_target_pairs={{0,8},{8,0},{2,10},{10,2},{4,12},{12,4},{6,14},{14,6},{16,24},{24,... | collective-permute-start | bytes 786440 | tf_op jit(solution)/shard_map/ppermute | solution.py:31
  17.5 8.6 %collective-permute-start.4 = (bf16[256,512]{1,0:T(8,128)(2,1)S(1)}, bf16[256,512]{1,0:T(8,128)(2,1)S(1)}, u32[]{:S(2)}, u32[]{:S(2)}) collective-permute-start(bf16[256,512]{1,0:T(8,128)(2,1)S(1)} %get-tuple-element.35.own_ref), channel_id=1, source_target_pairs={{0,1},{1,0},{2,3},{3,2},{4,5},{5,4},{6,7},{7,6},{8,9},{9,8},{10,11... | collective-permute-start | bytes 786440 | tf_op jit(solution)/shard_map/ppermute | solution.py:31
  19.8 9.2 %collective-permute-start.7 = (bf16[256,512]{1,0:T(8,128)(2,1)S(1)}, bf16[256,512]{1,0:T(8,128)(2,1)S(1)}, u32[]{:S(2)}, u32[]{:S(2)}) collective-permute-start(bf16[256,512]{1,0:T(8,128)(2,1)S(1)} %send_body.5.sent_ref.rest_1_), channel_id=1, source_target_pairs={{0,8},{8,0},{2,10},{10,2},{4,12},{12,4},{6,14},{14,6},{16,24},{24,... | collective-permute-start | bytes 786440 | tf_op jit(solution)/shard_map/ppermute | solution.py:31
  22.6 8.9 %collective-permute-start.6 = (bf16[256,512]{1,0:T(8,128)(2,1)S(1)}, bf16[256,512]{1,0:T(8,128)(2,1)S(1)}, u32[]{:S(2)}, u32[]{:S(2)}) collective-permute-start(bf16[256,512]{1,0:T(8,128)(2,1)S(1)} %get-tuple-element.38.own_ref), channel_id=1, source_target_pairs={{0,1},{1,0},{2,3},{3,2},{4,5},{5,4},{6,7},{7,6},{8,9},{9,8},{10,11... | collective-permute-start | bytes 786440 | tf_op jit(solution)/shard_map/ppermute | solution.py:31
  26.2 7.3 %collective-permute-start.8 = (bf16[256,512]{1,0:T(8,128)(2,1)S(1)}, bf16[256,512]{1,0:T(8,128)(2,1)S(1)}, u32[]{:S(2)}, u32[]{:S(2)}) collective-permute-start(bf16[256,512]{1,0:T(8,128)(2,1)S(1)} %send_body.6.sent_ref.rest_2_), channel_id=1, source_target_pairs={{0,8},{8,0},{2,10},{10,2},{4,12},{12,4},{6,14},{14,6},{16,24},{24,... | collective-permute-start | bytes 786440 | tf_op jit(solution)/shard_map/ppermute | solution.py:31
  27.5 7.1 %collective-permute-start.1 = (bf16[128,512]{1,0:T(8,128)(2,1)S(1)}, bf16[128,512]{1,0:T(8,128)(2,1)S(1)}, u32[]{:S(2)}, u32[]{:S(2)}) collective-permute-start(bf16[128,512]{1,0:T(8,128)(2,1)S(1)} %get-tuple-element.30), channel_id=1, source_target_pairs={{0,1},{1,0},{2,3},{3,2},{4,5},{5,4},{6,7},{7,6},{8,9},{9,8},{10,11... | collective-permute-start | bytes 393224 | tf_op jit(solution)/shard_map/ppermute | solution.py:31
  31.6 6.7 %collective-permute-start.9 = (bf16[256,512]{1,0:T(8,128)(2,1)S(1)}, bf16[256,512]{1,0:T(8,128)(2,1)S(1)}, u32[]{:S(2)}, u32[]{:S(2)}) collective-permute-start(bf16[256,512]{1,0:T(8,128)(2,1)S(1)} %send_body.7.rest_3_.sent_ref), channel_id=1, source_target_pairs={{0,8},{8,0},{2,10},{10,2},{4,12},{12,4},{6,14},{14,6},{16,24},{24,... | collective-permute-start | bytes 786440 | tf_op jit(solution)/shard_map/ppermute | solution.py:31
